TPU v7x, 512 devices: a whole 4x4x16 slice. The times are simulated.
512 devices in a mesh: segment: 4 (over z_lo), tm: 32 (over z_hi, y, core), dp: 4 (over x).
Axes of the slice: x: 4, y: 4, z: 16 (z_hi: 4, z_lo: 4; z = z_hi * 4 + z_lo), core: 2. Of those that a mesh axis runs over, the one named last changes fastest.
Arguments:
- features: bfloat16 [8, 128, 3, 8, 128], P('dp', 'tm'), may hold values from -6 to 6
- score_cot: float32 [8, 128, 3, 8], P('dp', 'tm'), may hold values from -6 to 6
- clip_frames: int32 [8], P('dp'), may hold values from 1 to 128, 768 in all
- conv_weights: bfloat16 [4, 2, 3456, 128], P('segment'), may hold values from -0.109375 to 0.109375
- norm_gains: float32 [4, 128], P('segment'), may hold values from 0.1 to 1.9
- score_head: float32 [128], replicated, may hold values from -0.5 to 0.5
Outputs:
- section_outputs: bfloat16 [4, 8, 128, 3, 8, 128], P('segment', 'dp', 'tm')
- weight_grads: bfloat16 [4, 2, 3456, 128], P('segment')
- section_input_grads: bfloat16 [4, 8, 128, 3, 8, 128], P('segment', 'dp', 'tm')
Inputs may be any that keep to these rules, and one draw needn't show every extreme that they name: `clip_frames`: the longest clip has exactly 128 frames; the entries sum to 768.
All inputs are finite; a program needn't handle non-finite values. No bound on the sum of `clip_frames` on one device may be relied on, other than what follows from the above.
Results may differ from a plain program's by a relative error of at most 0.017.
Values may be sent and summed in bfloat16 or wider, within the bound.
A program may use at most 64 MiB of HBM per device.

v0:
```python
import jax
import jax.numpy as jnp
from jax import lax
from jax.sharding import PartitionSpec as P

norm_eps = 1e-06


def passed_along(value, axis, steps):
    count = lax.axis_size(axis)
    leading, last = (max(0, -steps), min(count, count - steps))
    return lax.ppermute(value, axis, [(source, source + steps) for source in range(leading, last)])


def patches(extended, frames):
    height = extended.shape[1]
    breadth = extended.shape[2]
    padded = jnp.pad(extended, ((0, 0), (1, 1), (1, 1), (0, 0)))
    pieces = []
    for tap_time in range(3):
        for tap_row in range(3):
            for tap_col in range(3):
                pieces.append(
                    padded[
                        tap_time : tap_time + frames,
                        tap_row : tap_row + height,
                        tap_col : tap_col + breadth,
                    ]
                )
    return jnp.concatenate(pieces, axis=-1).reshape(frames * height * breadth, -1)


def convolve(extended, kernel, frames):
    columns = patches(extended, frames)
    result = jnp.dot(columns, kernel, preferred_element_type=jnp.float32)
    return result.reshape(frames, extended.shape[1], extended.shape[2], kernel.shape[1])


def transpose_conv(cotangent, flipped):
    frames = cotangent.shape[0]
    widened = jnp.pad(cotangent, ((2, 2), (0, 0), (0, 0), (0, 0)))
    return convolve(widened, flipped, frames + 2)


def kernel_grad(extended, cotangent):
    frames = cotangent.shape[0]
    columns = patches(extended, frames)
    flat_cot = cotangent.reshape(-1, cotangent.shape[-1])
    return lax.dot_general(
        columns, flat_cot, (((0,), (0,)), ((), ())), preferred_element_type=jnp.float32
    )


def flip_kernel(kernel):
    channels = kernel.shape[1]
    shaped = kernel.reshape(3, 3, 3, channels, channels)
    return jnp.transpose(shaped[::-1, ::-1, ::-1], (0, 1, 2, 4, 3)).reshape(27 * channels, channels)


def normalize(values, norm_gain):
    wide_values = values.astype(jnp.float32)
    inv_root = lax.rsqrt(jnp.mean(wide_values * wide_values, axis=-1, keepdims=True) + norm_eps)
    return (wide_values * inv_root * norm_gain).astype(jnp.bfloat16)


def norm_back(values, norm_gain, normed_cot):
    wide_values = values.astype(jnp.float32)
    inv_root = lax.rsqrt(jnp.mean(wide_values * wide_values, axis=-1, keepdims=True) + norm_eps)
    weighted = normed_cot * norm_gain
    inner = jnp.mean(weighted * wide_values, axis=-1, keepdims=True)
    return inv_root * weighted - wide_values * inv_root * inv_root * inv_root * inner


def silu_slope(pre_act):
    sig_value = jax.nn.sigmoid(pre_act)
    return sig_value * (1.0 + pre_act * (1.0 - sig_value))


def forward_block(block_in, norm_gain, first_kernel, second_kernel):
    frames = block_in.shape[0]
    normed = normalize(block_in, norm_gain)
    rim_frames = passed_along(normed[frames - 2 :], "tm", 1)
    normed_ext = jnp.concatenate([rim_frames, normed], axis=0)
    pre_act = convolve(normed_ext, first_kernel, frames)
    hidden = jax.nn.silu(pre_act).astype(jnp.bfloat16)
    hidden_edge = passed_along(hidden[frames - 2 :], "tm", 1)
    hidden_ext = jnp.concatenate([hidden_edge, hidden], axis=0)
    second = convolve(hidden_ext, second_kernel, frames)
    block_out = (block_in.astype(jnp.float32) + second).astype(jnp.bfloat16)
    return (block_out, (block_in, normed_ext, pre_act, hidden_ext))


def backward_block(grad_out, saved_set, norm_gain, first_flip, second_flip):
    block_in, normed_ext, pre_act, hidden_ext = saved_set
    frames = grad_out.shape[0]
    second_grad = kernel_grad(hidden_ext, grad_out)
    hidden_cot = transpose_conv(grad_out, second_flip)
    hidden_back = passed_along(hidden_cot[:2], "tm", -1)
    hidden_sum = hidden_cot[2:].at[frames - 2 :].add(hidden_back)
    pre_cot = (hidden_sum * silu_slope(pre_act)).astype(jnp.bfloat16)
    first_grad = kernel_grad(normed_ext, pre_cot)
    normed_cot = transpose_conv(pre_cot, first_flip)
    normed_back = passed_along(normed_cot[:2], "tm", -1)
    normed_sum = normed_cot[2:].at[frames - 2 :].add(normed_back)
    grad_in = (grad_out.astype(jnp.float32) + norm_back(block_in, norm_gain, normed_sum)).astype(
        jnp.bfloat16
    )
    return (grad_in, jnp.stack([first_grad, second_grad]))


def body(features, score_cot, clip_frames, conv_weights, norm_gains, score_head):
    segments = lax.axis_size("segment")
    segment_index = lax.axis_index("segment")
    micro_count = features.shape[0]
    frames = features.shape[1]
    tick_count = micro_count + segments - 1
    first_kernel = conv_weights[0, 0]
    second_kernel = conv_weights[0, 1]
    norm_gain = norm_gains[0]
    empty_clip = jnp.zeros(features.shape[1:], jnp.bfloat16)
    incoming = empty_clip
    tick_outputs = []
    tick_saves = []
    for tick_index in range(tick_count):
        fresh_clip = features[tick_index] if tick_index < micro_count else empty_clip
        block_in = jnp.where(segment_index == 0, fresh_clip, incoming)
        block_out, saved_set = forward_block(block_in, norm_gain, first_kernel, second_kernel)
        tick_outputs.append(block_out)
        tick_saves.append(saved_set)
        if tick_index + 1 < tick_count:
            incoming = passed_along(block_out, "segment", 1)
    section = lax.dynamic_slice_in_dim(jnp.stack(tick_outputs), segment_index, micro_count, 0)
    saved_stacks = tuple(
        (jnp.stack([saved_entry[member] for saved_entry in tick_saves]) for member in range(4))
    )
    frame_ids = lax.axis_index("tm") * frames + jnp.arange(frames, dtype=jnp.int32)
    valid_frames = (frame_ids[None, :] < clip_frames[:, None]).astype(jnp.float32)
    seed_grads = ((score_cot * valid_frames[:, :, None, None])[..., None] * score_head).astype(
        jnp.bfloat16
    )
    first_flip = flip_kernel(first_kernel)
    second_flip = flip_kernel(second_kernel)
    last_segment = segments - 1
    incoming_grad = empty_clip
    grad_total = jnp.zeros((2,) + first_kernel.shape, jnp.float32)
    tick_inputs = []
    for tick_index in range(tick_count):
        micro_index = tick_index - last_segment + segment_index
        is_valid = (micro_index >= 0) & (micro_index < micro_count)
        forward_tick = jnp.clip(micro_index + segment_index, 0, tick_count - 1)
        saved_set = tuple(
            (
                lax.dynamic_index_in_dim(saved_stack, forward_tick, 0, keepdims=False)
                for saved_stack in saved_stacks
            )
        )
        seed_grad = lax.dynamic_index_in_dim(
            seed_grads, jnp.clip(micro_index, 0, micro_count - 1), 0, keepdims=False
        )
        seed_grad = jnp.where(is_valid, seed_grad, jnp.zeros_like(seed_grad))
        grad_out = jnp.where(segment_index == last_segment, seed_grad, incoming_grad)
        grad_in, tick_grad = backward_block(grad_out, saved_set, norm_gain, first_flip, second_flip)
        grad_total = grad_total + tick_grad
        tick_inputs.append(grad_in)
        if tick_index + 1 < tick_count:
            incoming_grad = passed_along(grad_in, "segment", -1)
    input_grads = lax.dynamic_slice_in_dim(
        jnp.stack(tick_inputs), last_segment - segment_index, micro_count, 0
    )
    summed = lax.psum(grad_total, ("tm", "dp")).astype(jnp.bfloat16)
    return (section[None], summed[None], input_grads[None])


def solution(mesh):
    placed = (
        P("dp", "tm", None, None, None),
        P("dp", "tm", None, None),
        P("dp"),
        P("segment", None, None, None),
        P("segment", None),
        P(),
    )
    return jax.shard_map(
        body,
        mesh=mesh,
        in_specs=placed,
        out_specs=(
            P("segment", "dp", "tm", None, None, None),
            P("segment", None, None, None),
            P("segment", "dp", "tm", None, None, None),
        ),
        check_vma=False,
    )
```

profile of v0, /device:TPU:288, one launch (start us, length us, event | category | flops | bytes accessed | tf_op | source)
XLA Modules:
  0.0 1152.0 jit_solution(4451219014522414663)
XLA Ops:
  30.2 9.6 collective-permute-start.14
  49.5 9.2 collective-permute-done.1
  59.6 2.8 collective-permute-start.2
  67.5 9.1 collective-permute-done.3
  79.6 9.1 collective-permute-done.4
  89.6 2.8 collective-permute-start.5
  92.4 2.9 collective-permute-done.5
  97.5 9.1 collective-permute-done.6
  109.6 9.1 collective-permute-done.7
  119.6 2.8 collective-permute-start.8
  122.4 2.9 collective-permute-done.8
  127.4 9.1 collective-permute-done.9
  139.5 9.1 collective-permute-done.10
  149.5 2.8 collective-permute-start.11
  152.3 2.9 collective-permute-done.11
  157.6 8.9 collective-permute-done.12
  172.9 9.7 collective-permute-start.15
  190.6 3.8 collective-permute-done.16
  195.5 5.2 collective-permute-start.17
  203.3 9.8 collective-permute-start.18
  216.9 3.7 collective-permute-done.19
  221.7 8.7 collective-permute-start.20
  232.8 9.7 collective-permute-start.21
  244.3 2.4 collective-permute-start.22
  247.2 2.8 collective-permute-done.22
  251.1 8.5 collective-permute-start.23
  262.3 9.7 collective-permute-start.24
  273.7 3.1 collective-permute-start.25
  277.3 2.1 collective-permute-done.25
  280.5 8.6 collective-permute-start.26
  292.4 9.6 collective-permute-start.27
  303.3 843.4 %all-reduce.41 = bf16[2,3456,128]{2,1,0:T(8,128)(2,1)} all-reduce(f32[2,3456,128]{2,1,0:T(8,128)S(1)} %fusion.2), channel_id=1, replica_groups=mesh['segment'=4,'tm'=32,'dp'=4] {'tm','dp'}, use_global_device_ids=true, to_apply=%region_13.14 | all-reduce | flops 884736 | bytes 5308416 | tf_op jit(solution)/shard_map/psum | solution.py:170
  (1024 shorter events, 103.7 us)
Async XLA Ops:
  0.6 24.2 %copy-start = (bf16[1,2,3456,128]{3,2,1,0:T(8,128)(2,1)S(1)}, bf16[1,2,3456,128]{3,2,1,0:T(8,128)(2,1)}, u32[]{:S(2)}) copy-start(bf16[1,2,3456,128]{3,2,1,0:T(8,128)(2,1)} %param.29) | copy-start | bytes 5308420
  3.1 40.4 %collective-permute-start = (bf16[2,3,8,128]{3,2,1,0:T(8,128)(2,1)}, bf16[2,3,8,128]{3,2,1,0:T(8,128)(2,1)S(1)}, u32[]{:S(2)}, u32[]{:S(2)}) collective-permute-start(bf16[2,3,8,128]{3,2,1,0:T(8,128)(2,1)} %slice.3956), channel_id=1, source_target_pairs={{0,4},{4,8},{8,12},{12,16},{16,20},{20,24},{24,28},{28,32},{32,36}... | collective-permute-start | bytes 36872 | tf_op jit(solution)/shard_map/ppermute | solution.py:12
  7.9 16.3 %copy-start.8 = (bf16[4,3,8,128]{3,2,1,0:T(8,128)(2,1)}, bf16[4,3,8,128]{3,2,1,0:T(8,128)(2,1)S(1)}, u32[]{:S(2)}) copy-start(bf16[4,3,8,128]{3,2,1,0:T(8,128)(2,1)S(1)} %select_bitcast_fusion) | copy-start | bytes 73732
  30.2 32.3 %collective-permute-start.14 = (f32[2,3,8,128]{3,2,1,0:T(8,128)}, f32[2,3,8,128]{3,2,1,0:T(8,128)}, u32[]{:S(2)}, u32[]{:S(2)}) collective-permute-start(f32[2,3,8,128]{3,2,1,0:T(8,128)} %bitcast.42), channel_id=1, source_target_pairs={{4,0},{8,4},{12,8},{16,12},{20,16},{24,20},{28,24},{32,28},{36,32}... | collective-permute-start | bytes 73736 | tf_op jit(solution)/shard_map/ppermute | solution.py:12
  47.5 11.2 collective-permute-start.1
  49.5 15.8 %copy-start.1 = (bf16[5,4,3,8,128]{4,3,2,1,0:T(8,128)(2,1)S(1)}, bf16[5,4,3,8,128]{4,3,2,1,0:T(8,128)(2,1)}, u32[]{:S(2)}) copy-start(bf16[5,4,3,8,128]{4,3,2,1,0:T(8,128)(2,1)} %constant_dynamic-update-slice_fusion.402) | copy-start | bytes 368644
  59.6 5.7 collective-permute-start.2
  65.6 11.0 collective-permute-start.3
  77.7 11.0 collective-permute-start.4
  89.6 5.7 collective-permute-start.5
  95.5 11.0 collective-permute-start.6
  107.6 11.0 collective-permute-start.7
  119.6 5.7 collective-permute-start.8
  125.5 11.0 collective-permute-start.9
  137.6 11.0 collective-permute-start.10
  149.5 5.7 collective-permute-start.11
  155.5 11.0 collective-permute-start.12
  157.6 116.0 %copy-start.2 = (bf16[5,4,3,8,128]{4,3,2,1,0:T(8,128)(2,1)}, bf16[5,4,3,8,128]{4,3,2,1,0:T(8,128)(2,1)S(1)}, u32[]{:S(2)}) copy-start(bf16[5,4,3,8,128]{4,3,2,1,0:T(8,128)(2,1)S(1)} %constant_dynamic-update-slice_fusion.398) | copy-start | bytes 368644
  169.7 12.8 %collective-permute-start.13 = (bf16[2,3,8,128]{3,2,1,0:T(8,128)(2,1)S(1)}, bf16[2,3,8,128]{3,2,1,0:T(8,128)(2,1)S(1)}, u32[]{:S(2)}, u32[]{:S(2)}) collective-permute-start(bf16[2,3,8,128]{3,2,1,0:T(8,128)(2,1)S(1)} %slice.4001), channel_id=1, source_target_pairs={{0,4},{4,8},{8,12},{12,16},{16,20},{20,24},{24,28},{28,32},{32,36}... | collective-permute-start | bytes 36872 | tf_op jit(solution)/shard_map/ppermute | solution.py:12
  172.9 15.4 %collective-permute-start.15 = (f32[2,3,8,128]{3,2,1,0:T(8,128)S(1)}, f32[2,3,8,128]{3,2,1,0:T(8,128)S(1)}, u32[]{:S(2)}, u32[]{:S(2)}) collective-permute-start(f32[2,3,8,128]{3,2,1,0:T(8,128)S(1)} %bitcast.632), channel_id=1, source_target_pairs={{4,0},{8,4},{12,8},{16,12},{20,16},{24,20},{28,24},{32,28},{36,32}... | collective-permute-start | bytes 73736 | tf_op jit(solution)/shard_map/ppermute | solution.py:12
  188.6 5.7 collective-permute-start.16
  195.5 6.7 collective-permute-start.17
  203.3 11.3 collective-permute-start.18
  214.9 5.7 collective-permute-start.19
  221.7 10.0 collective-permute-start.20
  232.8 11.2 collective-permute-start.21
  244.3 5.7 collective-permute-start.22
  251.1 10.0 collective-permute-start.23
  262.3 11.2 collective-permute-start.24
  273.7 5.7 collective-permute-start.25
  280.5 10.1 collective-permute-start.26
  292.4 855.2 %collective-permute-start.27 = (f32[2,3,8,128]{3,2,1,0:T(8,128)}, f32[2,3,8,128]{3,2,1,0:T(8,128)}, u32[]{:S(2)}, u32[]{:S(2)}) collective-permute-start(f32[2,3,8,128]{3,2,1,0:T(8,128)} %bitcast.185), channel_id=1, source_target_pairs={{4,0},{8,4},{12,8},{16,12},{20,16},{24,20},{28,24},{32,28},{36,32}... | collective-permute-start | bytes 73736 | tf_op jit(solution)/shard_map/ppermute | solution.py:12
  (17 other events, 120.0 us)
where the time goes:
time: 1150 us
  blocking collectives  843 us (73%)
  starting transfers between devices  129 us (11%)
  waiting for transfers between devices  104 us (9%)
  local copies, waits for them, and re-layouts  41.3 us (4%)
  other arithmetic  15.4 us (1%)
  matrix products  13.7 us (1%)
    psum x1, blocking collectives, body(): summed = lax.psum(grad_total, ('tm', 'dp')).astype(jnp.bfloat16)  843 us
    ppermute x28, starting transfers between devices, passed_along(): lax.ppermute(value, axis, [(source, source + steps) for source in range(l...  129 us
    ppermute x28, waiting for transfers between devices, passed_along(): lax.ppermute(value, axis, [(source, source + steps) for source in range(l...  104 us
    unnamed x767, local copies, waits for them, and re-layouts  29.1 us
  transfers between devices with their start and end apart: 28, of which 23 were waited for; matrix products, arithmetic and copies ran while one was open for 4% of the time, Pallas kernels for 0%

commit v1 on v0

v1 whole, which is shorter than its diff:
```python
import functools

import jax
import jax.numpy as jnp
from jax import lax
from jax.experimental import pallas as pl
from jax.experimental.pallas import tpu as pltpu
from jax.sharding import PartitionSpec as P

norm_eps = 1e-06
FRAMES_HERE = 4
GROUP = 7
BAND = 32
BF, F32 = jnp.bfloat16, jnp.float32


def column_shifts(values):
    shape = values.shape
    flat = values.reshape(-1, 8, 128)
    column = lax.broadcasted_iota(jnp.int32, flat.shape, 1)
    before = jnp.where(column == 0, 0.0, pltpu.roll(flat, 1, 1))
    after = jnp.where(column == 7, 0.0, pltpu.roll(flat, 7, 1))
    return [before.reshape(shape), values, after.reshape(shape)]


def fill(patch_ref, values):
    frames = values.shape[0]
    for e, shifted in enumerate(column_shifts(values)):
        patch_ref[:frames, 1:4, :, e * 128 : (e + 1) * 128] = shifted.astype(BF)


def convolve(patch_ref, weight_ref, which, frames):
    total = None
    for a in range(3):
        for b in range(3):
            rows = patch_ref[a : a + frames, b : b + 3].reshape(frames * 48, 384)
            taps = weight_ref[which, (9 * a + 3 * b) * 128 : (9 * a + 3 * b + 3) * 128, :]
            part = jnp.dot(rows, taps, preferred_element_type=F32)
            total = part if total is None else total + part
    return total.reshape(frames, 3, 16, 128)


def kernel(
    S, T, Y, Z,
    feat_ref, score_ref, clip_ref, weight_hbm, gain_ref, head_ref,
    out_ref, grad_ref, back_ref,
    weight, flipped, xin, din, slope, patch8, patch6, vsend, vbuf, vt, upad, pcot, gsend, r1, s1, r2, zbuf,
    local_sem, send_sem, recv_sem,
):
    seg, t, x = lax.axis_index("segment"), lax.axis_index("tm"), lax.axis_index("dp")
    core = lax.rem(t, 2)
    y = lax.rem(t // 2, Y)
    z = t // (2 * Y)
    frames = FRAMES_HERE

    def time_of(z, y, core):
        return (z * Y + y) * 2 + core

    def to(seg_to, t_to, x_to):
        return {"segment": seg_to, "tm": t_to, "dp": x_to}

    def remote(source, target, send, recv, device):
        return pltpu.make_async_remote_copy(
            src_ref=source, dst_ref=target, send_sem=send_sem.at[send], recv_sem=recv_sem.at[recv],
            device_id=device, device_id_type=pl.DeviceIdType.MESH,
        )

    load = pltpu.make_async_copy(weight_hbm.at[0], weight, local_sem)
    load.start()

    patch8[:, 0] = jnp.zeros_like(patch8[:, 0])
    patch8[:, 4] = jnp.zeros_like(patch8[:, 4])
    patch6[:, 0] = jnp.zeros_like(patch6[:, 0])
    patch6[:, 4] = jnp.zeros_like(patch6[:, 4])
    upad[...] = jnp.zeros_like(upad)
    gsend[27] = jnp.zeros_like(gsend[27])
    has_before, has_after = t > 0, t < T - 1
    below, above = seg > 0, seg < S - 1
    before, after = jnp.maximum(t - 1, 0), jnp.minimum(t + 1, T - 1)
    lower, upper = jnp.maximum(seg - 1, 0), jnp.minimum(seg + 1, S - 1)

    @pl.when(jnp.logical_not(has_before))
    def _():
        xin[0:frames] = jnp.zeros_like(xin[0:frames])

    @pl.when(jnp.logical_not(has_after))
    def _():
        din[frames:] = jnp.zeros_like(din[frames:])
        slope[frames:] = jnp.zeros_like(slope[frames:])

    barrier = pltpu.get_barrier_semaphore()
    expected = 9
    for condition, device in (
        (has_before, to(seg, before, x)),
        (has_after, to(seg, after, x)),
        (above, to(upper, t, x)),
        (jnp.logical_and(above, has_after), to(upper, after, x)),
        (below, to(lower, t, x)),
        (jnp.logical_and(below, has_before), to(lower, before, x)),
    ):
        expected = expected + condition.astype(jnp.int32)

        @pl.when(condition)
        def _(device=device):
            pl.semaphore_signal(barrier, 1, device_id=device, device_id_type=pl.DeviceIdType.MESH)

    for step in range(1, 4):
        for device in (
            to(seg, t, lax.rem(x + step, 4)),
            to(seg, time_of(z, lax.rem(y + step, 4), core), x),
            to(seg, time_of(lax.rem(z + step, 4), y, core), x),
        ):
            pl.semaphore_signal(barrier, 1, device_id=device, device_id_type=pl.DeviceIdType.MESH)

    def own_features():
        return jnp.concatenate([feat_ref[0].astype(F32), feat_ref[1].astype(F32)], axis=2)

    @pl.when(seg == 0)
    def _():
        xin[frames:] = own_features().astype(BF)

    @pl.when(seg == S - 1)
    def _():
        eye = lax.broadcasted_iota(jnp.int32, (8, 8), 0) == lax.broadcasted_iota(jnp.int32, (8, 8), 1)
        head = head_ref[...]
        for f in range(frames):
            for i in range(3):
                halves = []
                for n in range(2):
                    line = score_ref[n, f, i : i + 1, :]
                    valid = jnp.where(t * frames + f < clip_ref[n], 1.0, 0.0)
                    stood = jnp.sum(jnp.where(eye, jnp.broadcast_to(line, (8, 8)), 0.0), axis=1, keepdims=True)
                    halves.append((stood * valid) * head)
                din[f, i] = jnp.concatenate(halves, axis=0).astype(BF)

    pl.semaphore_wait(barrier, expected)

    own_x = remote(xin.at[pl.ds(frames, frames)], xin.at[pl.ds(0, frames)], 0, 0, to(seg, after, x))
    own_d = remote(din.at[pl.ds(0, frames)], din.at[pl.ds(frames, frames)], 1, 1, to(seg, before, x))
    x_up = remote(out_ref, xin.at[pl.ds(frames, frames)], 2, 2, to(upper, t, x))
    x_up_after = remote(out_ref, xin.at[pl.ds(0, frames)], 23, 0, to(upper, after, x))
    d_down = remote(back_ref, din.at[pl.ds(0, frames)], 3, 3, to(lower, t, x))
    d_down_before = remote(back_ref, din.at[pl.ds(frames, frames)], 24, 1, to(lower, before, x))
    slope_back = remote(slope.at[pl.ds(0, 2)], slope.at[pl.ds(4, 2)], 4, 4, to(seg, before, x))
    partner = to(seg, t + 1 - 2 * core, x)
    v_swap = remote(vsend, vbuf.at[pl.ds(6 * core, 4)], 5, 5, partner)
    u_to_one = remote(din.at[pl.ds(0, 4)], upad.at[pl.ds(2, 4), pl.ds(1, 3)], 6, 6, partner)
    u_to_zero = remote(pcot, upad.at[pl.ds(8, 2), pl.ds(1, 3)], 6, 6, partner)

    @pl.when(jnp.logical_and(seg == 0, has_after))
    def _():
        own_x.start()

    @pl.when(jnp.logical_and(seg == S - 1, has_before))
    def _():
        own_d.start()

    load.wait()

    def flip_all():
        def one(i, carry):
            source = pl.multiple_of(i * 128, 128)
            target = pl.multiple_of((26 - i) * 128, 128)
            for which in range(2):
                tap = weight[which, pl.ds(source, 128), :].astype(F32)
                flipped[which, pl.ds(target, 128), :] = tap.T.astype(BF)
            return carry

        lax.fori_loop(0, 27, one, 0)

    @pl.when(below)
    def _():
        flip_all()

    @pl.when(below)
    def _():
        x_up.wait_recv()

    @pl.when(has_before)
    def _():
        x_up_after.wait_recv()

    gain = gain_ref[...]
    wide = xin[...].astype(F32)
    root = lax.rsqrt(jnp.mean(wide * wide, axis=-1, keepdims=True) + norm_eps)
    normed = (wide * root * gain).astype(BF).astype(F32)
    fill(patch8, normed)
    pre = convolve(patch8, weight, 0, 6)
    sig = 1.0 / (1.0 + jnp.exp(-pre))
    hidden = (pre * sig).astype(BF).astype(F32)
    slope[0:4] = (sig * (1.0 + pre * (1.0 - sig)))[2:6]

    @pl.when(has_before)
    def _():
        slope_back.start()

    fill(patch6, hidden)
    vsend[...] = jnp.where(core == 0, hidden[0:4], normed[4:8]).astype(BF)
    vbuf[pl.ds(4 * core, 6)] = jnp.where(core == 0, normed[2:8], hidden).astype(BF)
    v_swap.start()
    second = convolve(patch6, weight, 1, 4)
    out_ref[...] = (xin[4:8].astype(F32) + second).astype(BF)

    @pl.when(above)
    def _():
        x_up.start()

    @pl.when(jnp.logical_and(above, has_after))
    def _():
        x_up_after.start()

    def stand_up():
        v_swap.wait_recv()
        flat = vbuf[...].astype(F32)
        for e, shifted in enumerate(column_shifts(flat)):
            rows = jnp.concatenate([shifted.reshape(480, 128), jnp.zeros((32, 128), F32)], axis=0)
            vt[e * 128 : (e + 1) * 128, :] = rows.T.astype(BF)

    @pl.when(seg == 0)
    def _():
        flip_all()

    @pl.when(above)
    def _():
        stand_up()

    @pl.when(above)
    def _():
        d_down.wait_recv()

    @pl.when(core == 0)
    def _():
        u_to_one.start()

    @pl.when(core == 1)
    def _():
        upad[6:10, 1:4] = din[0:4]

    @pl.when(has_after)
    def _():
        d_down_before.wait_recv()

    fill(patch8, din[...].astype(F32))
    hidden_cot = convolve(patch8, flipped, 1, 6)

    @pl.when(has_after)
    def _():
        slope_back.wait_recv()

    pre_cot = (hidden_cot * slope[...]).astype(BF)

    @pl.when(core == 0)
    def _():
        upad[2:8, 1:4] = pre_cot

    @pl.when(core == 1)
    def _():
        pcot[...] = pre_cot[2:4]
        u_to_zero.start()

    fill(patch6, pre_cot.astype(F32))
    normed_cot = convolve(patch6, flipped, 0, 4)
    wide = xin[4:8].astype(F32)
    root = lax.rsqrt(jnp.mean(wide * wide, axis=-1, keepdims=True) + norm_eps)
    weighted = normed_cot * gain
    inner = jnp.mean(weighted * wide, axis=-1, keepdims=True)
    back_ref[...] = (din[0:4].astype(F32) + (root * weighted - wide * root * root * root * inner)).astype(BF)

    @pl.when(below)
    def _():
        d_down.start()

    @pl.when(jnp.logical_and(below, has_before))
    def _():
        d_down_before.start()

    @pl.when(seg == S - 1)
    def _():
        stand_up()

    first, other = jnp.where(core == 0, x, y), jnp.where(core == 0, y, x)

    def on_first(step):
        turned = lax.rem(first + step, 4)
        return to(seg, time_of(z, jnp.where(core == 0, y, turned), core), jnp.where(core == 0, turned, x))

    def on_other(step):
        turned = lax.rem(other + step, 4)
        return to(seg, time_of(z, jnp.where(core == 0, turned, y), core), jnp.where(core == 0, x, turned))

    def group_at(step):
        return pl.ds(lax.rem(first + step, 4) * GROUP, GROUP)

    def band_at(step):
        return pl.ds(pl.multiple_of(lax.rem(other + step, 4) * BAND, BAND), BAND)

    @pl.when(core == 0)
    def _():
        u_to_zero.wait_recv()

    @pl.when(core == 1)
    def _():
        u_to_one.wait_recv()

    for a in range(3):
        for b in range(3):
            rows = upad[2 - a : 12 - a, 2 - b : 5 - b].reshape(480, 128)
            rows = jnp.concatenate([rows, jnp.zeros((32, 128), BF)], axis=0)
            part = jnp.dot(vt[...], rows, preferred_element_type=F32)
            gsend[9 * a + 3 * b : 9 * a + 3 * b + 3] = part.astype(BF).reshape(3, 128, 128)

    round1 = [remote(gsend.at[group_at(k)], r1.at[k - 1], 7 + k, 7 + k, on_first(k)) for k in range(1, 4)]
    for copy in round1:
        copy.start()
    total = gsend[group_at(0)].astype(F32)
    for k in range(3):
        round1[k].wait_recv()
        total = total + r1[k].astype(F32)
    s1[...] = total.astype(BF)
    round2 = [remote(s1.at[:, band_at(k)], r2.at[k - 1], 10 + k, 10 + k, on_other(k)) for k in range(1, 4)]
    for copy in round2:
        copy.start()
    total = s1[:, band_at(0)].astype(F32)
    for k in range(3):
        round2[k].wait_recv()
        total = total + r2[k].astype(F32)
    zbuf[z] = total.astype(BF)
    round3 = [
        remote(zbuf.at[z], zbuf.at[z], 13 + k, 13 + k, to(seg, time_of(lax.rem(z + k, 4), y, core), x))
        for k in range(1, 4)
    ]
    for copy in round3:
        copy.start()
    for k in range(3):
        round3[k].wait_recv()
    total = zbuf[0].astype(F32) + zbuf[1].astype(F32) + zbuf[2].astype(F32) + zbuf[3].astype(F32)
    grad_ref[core, group_at(0), band_at(0)] = total.astype(BF)
    piece = grad_ref.at[core, group_at(0), band_at(0)]
    round4 = [remote(piece, piece, 16 + k, 16 + k, on_other(k)) for k in range(1, 4)]
    for copy in round4:
        copy.start()
    for copy in round4:
        copy.wait_recv()
    whole = grad_ref.at[core, group_at(0)]
    round5 = [remote(whole, whole, 19 + k, 19 + k, on_first(k)) for k in range(1, 4)]
    for copy in round5:
        copy.start()
    round6 = []
    for k in range(4):
        held = grad_ref.at[core, group_at((4 - k) % 4)]
        forward = remote(held, held, 25 + k, 23 + k, partner)
        if k > 0:
            round5[k - 1].wait_recv()
        forward.start()
        round6.append(forward)
    for copy in round6:
        copy.wait_recv()

    for copy in round1 + round2 + round3 + round4 + round5 + round6:
        copy.wait_send()
    v_swap.wait_send()

    @pl.when(core == 0)
    def _():
        u_to_one.wait_send()

    @pl.when(core == 1)
    def _():
        u_to_zero.wait_send()

    @pl.when(has_before)
    def _():
        slope_back.wait_send()

    @pl.when(jnp.logical_and(seg == 0, has_after))
    def _():
        own_x.wait_send()

    @pl.when(jnp.logical_and(seg == S - 1, has_before))
    def _():
        own_d.wait_send()

    @pl.when(above)
    def _():
        x_up.wait_send()

    @pl.when(jnp.logical_and(above, has_after))
    def _():
        x_up_after.wait_send()

    @pl.when(below)
    def _():
        d_down.wait_send()

    @pl.when(jnp.logical_and(below, has_before))
    def _():
        d_down_before.wait_send()


def solution(mesh):
    S, T = mesh.shape["segment"], mesh.shape["tm"]
    Y = 4
    Z = T // (2 * Y)
    vmem = pl.BlockSpec(memory_space=pltpu.VMEM)
    cells = (FRAMES_HERE, 3, 16, 128)

    def body(features, score_cot, clip_frames, conv_weights, norm_gains, score_head):
        out, grad, back = pl.pallas_call(
            functools.partial(kernel, S, T, Y, Z),
            out_shape=(
                jax.ShapeDtypeStruct(cells, BF),
                jax.ShapeDtypeStruct((2, 28, 128, 128), BF),
                jax.ShapeDtypeStruct(cells, BF),
            ),
            in_specs=[
                vmem, vmem, pl.BlockSpec(memory_space=pltpu.SMEM), pl.BlockSpec(memory_space=pl.ANY), vmem, vmem,
            ],
            out_specs=(vmem, vmem, vmem),
            scratch_shapes=[
                pltpu.VMEM((2, 3456, 128), BF),
                pltpu.VMEM((2, 3456, 128), BF),
                pltpu.VMEM((8, 3, 16, 128), BF),
                pltpu.VMEM((8, 3, 16, 128), BF),
                pltpu.VMEM((6, 3, 16, 128), F32),
                pltpu.VMEM((8, 5, 16, 384), BF),
                pltpu.VMEM((6, 5, 16, 384), BF),
                pltpu.VMEM((4, 3, 16, 128), BF),
                pltpu.VMEM((10, 3, 16, 128), BF),
                pltpu.VMEM((384, 512), BF),
                pltpu.VMEM((12, 5, 16, 128), BF),
                pltpu.VMEM((2, 3, 16, 128), BF),
                pltpu.VMEM((28, 128, 128), BF),
                pltpu.VMEM((3, GROUP, 128, 128), BF),
                pltpu.VMEM((GROUP, 128, 128), BF),
                pltpu.VMEM((3, GROUP, BAND, 128), BF),
                pltpu.VMEM((4, GROUP, BAND, 128), BF),
                pltpu.SemaphoreType.DMA,
                pltpu.SemaphoreType.DMA((29,)),
                pltpu.SemaphoreType.DMA((27,)),
            ],
            compiler_params=pltpu.CompilerParams(
                collective_id=0, has_side_effects=True, vmem_limit_bytes=40 * 1024 * 1024
            ),
            cost_estimate=pl.CostEstimate(flops=10**9, bytes_accessed=6 * 10**6, transcendentals=10**5),
        )(features, score_cot, clip_frames, conv_weights, norm_gains, score_head.reshape(1, 128))

        def split_clips(cells):
            return jnp.transpose(cells.reshape(FRAMES_HERE, 3, 2, 8, 128), (2, 0, 1, 3, 4))[None]

        return split_clips(out), grad[:, :27].reshape(1, 2, 3456, 128), split_clips(back)

    return jax.shard_map(
        body,
        mesh=mesh,
        in_specs=(
            P("dp", "tm", None, None, None),
            P("dp", "tm", None, None),
            P("dp"),
            P("segment", None, None, None),
            P("segment", None),
            P(),
        ),
        out_specs=(
            P("segment", "dp", "tm", None, None, None),
            P("segment", None, None, None),
            P("segment", "dp", "tm", None, None, None),
        ),
        check_vma=False,
    )
```

time: 1150 us -> 109 us (0.09)
  the two profiles are of different devices: /device:TPU:288 before, /device:TPU:1 now
where the time goes in v1:
time: 109 us
  Pallas kernels  101 us (93%)
  local copies, waits for them, and re-layouts  7.02 us (6%)
    pallas_call x1, Pallas kernels, body(): pl.pallas_call(functools.partial(kernel, S, T, Y, Z), out_shape=(jax.Shap...  101 us
    unnamed x11, local copies, waits for them, and re-layouts  4.95 us

profile of v1, /device:TPU:1, one launch (start us, length us, event | category | flops | bytes accessed | tf_op | source)
XLA Modules:
  0.0 109.0 jit_solution(12770175028599981201)
XLA Ops:
  0.6 0.7 copy.9.score_ref
  1.3 0.0 copy-start
  1.3 1.5 %copy-done = bf16[1,2,3456,128]{3,2,1,0:T(8,128)(2,1)S(1)} copy-done((bf16[1,2,3456,128]{3,2,1,0:T(8,128)(2,1)S(1)}, bf16[1,2,3456,128]{3,2,1,0:T(8,128)(2,1)}, u32[]{:S(2)}) %copy-start) | copy-done | bytes 1769496
  2.8 0.0 copy-start.1
  2.8 0.8 copy-done.1
  3.6 0.0 copy-start.2
  3.6 0.7 copy-done.2
  4.3 0.0 copy-start.3
  4.3 0.7 copy-done.3
  4.9 0.0 copy-start.4
  4.9 0.7 copy-done.4
  5.6 101.4 %shard_map.85 = (bf16[4,3,16,128]{3,2,1,0:T(8,128)(2,1)S(1)}, bf16[2,28,128,128]{3,2,1,0:T(8,128)(2,1)S(1)}, bf16[4,3,16,128]{3,2,1,0:T(8,128)(2,1)S(1)}) custom-call(bf16[2,4,3,8,128]{4,3,2,1,0:T(8,128)(2,1)S(1)} %copy-done.1, f32[2,4,3,8]{3,2,1,0:T(4,128)S(1)} %copy.9.score_ref, s32[2]{0:T(128)S(1)} %copy-done.2, bf16[1,2,3456,128]{3,2,1,0:T(8,128)(2,1)S(1)} %copy-done, ...), custom_call_target="tpu_custom_call" | custom-call | flops 1000000000 | bytes 6000000 | tf_op jit(solution)/shard_map/pallas_call | solution.py:408
  107.0 0.7 copy_bitcast_fusion
  107.6 1.4 %slice.3 = bf16[2,27,128,128]{3,2,1,0:T(8,128)(2,1)} slice(bf16[2,28,128,128]{3,2,1,0:T(8,128)(2,1)S(1)} %get-tuple-element.7), slice={[0:2], [0:27], [0:128], [0:128]} | slice | bytes 3538944 | tf_op jit(solution)/shard_map/slice | solution.py:450
Async XLA Ops:
  1.3 1.5 %copy-start = (bf16[1,2,3456,128]{3,2,1,0:T(8,128)(2,1)S(1)}, bf16[1,2,3456,128]{3,2,1,0:T(8,128)(2,1)}, u32[]{:S(2)}) copy-start(bf16[1,2,3456,128]{3,2,1,0:T(8,128)(2,1)} %weight_hbm.1) | copy-start | bytes 5308420
  2.8 0.8 copy-start.1
  3.6 0.7 copy-start.2
  4.3 0.7 copy-start.3
  4.9 0.7 copy-start.4

commit v2 on v1

v2 whole, which is shorter than its diff:
```python
import functools

import jax
import jax.numpy as jnp
from jax import lax
from jax.experimental import pallas as pl
from jax.experimental.pallas import tpu as pltpu
from jax.sharding import PartitionSpec as P

norm_eps = 1e-06
FRAMES_HERE = 4
GROUP = 7
BAND = 16
SENDS = 112
BF, F32 = jnp.bfloat16, jnp.float32


def column_shifts(values):
    shape = values.shape
    flat = values.reshape(-1, 8, 128)
    column = lax.broadcasted_iota(jnp.int32, flat.shape, 1)
    before = jnp.where(column == 0, 0.0, pltpu.roll(flat, 1, 1))
    after = jnp.where(column == 7, 0.0, pltpu.roll(flat, 7, 1))
    return [before.reshape(shape), values, after.reshape(shape)]


def fill(patch_ref, values):
    frames = values.shape[0]
    for e, shifted in enumerate(column_shifts(values)):
        patch_ref[:frames, 1:4, :, e * 128 : (e + 1) * 128] = shifted.astype(BF)


def convolve(patch_ref, weight_ref, which, frames, at=0):
    total = None
    for a in range(3):
        for b in range(3):
            rows = patch_ref[at + a : at + a + frames, b : b + 3].reshape(frames * 48, 384)
            taps = weight_ref[which, (9 * a + 3 * b) * 128 : (9 * a + 3 * b + 3) * 128, :]
            part = jnp.dot(rows, taps, preferred_element_type=F32)
            total = part if total is None else total + part
    return total.reshape(frames, 3, 16, 128)


def kernel(
    S, T, Y, Z,
    feat_hbm, score_hbm, clip_hbm, weight_hbm, gain_hbm, head_hbm,
    out_ref, grad_ref, back_ref,
    feat_ref, score_ref, clip_ref, gain_ref, head_ref, own, weight, flipped, xin, din, slope, patch8, patch6, vsend, vbuf, vt, upad, pcot, gsend, r1, s1, r2, zbuf,
    local_sem, send_sem, recv_sem, ready,
):
    seg, t, x = lax.axis_index("segment"), lax.axis_index("tm"), lax.axis_index("dp")
    core = lax.rem(t, 2)
    y = lax.rem(t // 2, Y)
    z = t // (2 * Y)
    frames = FRAMES_HERE

    def time_of(z, y, core):
        return (z * Y + y) * 2 + core

    def to(seg_to, t_to, x_to):
        return {"segment": seg_to, "tm": t_to, "dp": x_to}

    def remote(source, target, send, recv, device):
        return pltpu.make_async_remote_copy(
            src_ref=source, dst_ref=target, send_sem=send_sem.at[send], recv_sem=recv_sem.at[recv],
            device_id=device, device_id_type=pl.DeviceIdType.MESH,
        )

    loads = [
        pltpu.make_async_copy(source, target, local_sem.at[i])
        for i, (source, target) in enumerate((
            (feat_hbm, feat_ref), (gain_hbm, gain_ref), (weight_hbm.at[0], weight),
            (score_hbm, score_ref), (clip_hbm, clip_ref), (head_hbm, head_ref),
        ))
    ]
    for load in loads:
        load.start()

    patch8[:, 0] = jnp.zeros_like(patch8[:, 0])
    patch8[:, 4] = jnp.zeros_like(patch8[:, 4])
    patch6[:, 0] = jnp.zeros_like(patch6[:, 0])
    patch6[:, 4] = jnp.zeros_like(patch6[:, 4])
    upad[...] = jnp.zeros_like(upad)
    gsend[27] = jnp.zeros_like(gsend[27])
    has_before, has_after = t > 0, t < T - 1
    seam_after = jnp.logical_and(has_after, lax.rem(t, 2 * Y) == 2 * Y - 1)
    seam_before = jnp.logical_and(has_before, lax.rem(t, 2 * Y) == 0)
    bridge_after = jnp.logical_and(seg == S - 1, seam_after)
    bridge_before = jnp.logical_and(seg == 0, seam_before)
    below, above = seg > 0, seg < S - 1
    before, after = jnp.maximum(t - 1, 0), jnp.minimum(t + 1, T - 1)
    lower, upper = jnp.maximum(seg - 1, 0), jnp.minimum(seg + 1, S - 1)

    @pl.when(jnp.logical_not(has_before))
    def _():
        xin[0:frames] = jnp.zeros_like(xin[0:frames])

    @pl.when(jnp.logical_not(has_after))
    def _():
        din[frames:] = jnp.zeros_like(din[frames:])
        slope[frames:] = jnp.zeros_like(slope[frames:])

    barrier = pltpu.get_barrier_semaphore()
    expected = 8
    for condition, device in (
        (has_before, to(seg, before, x)),
        (has_after, to(seg, after, x)),
        (above, to(upper, t, x)),
        (jnp.logical_and(above, has_after), to(upper, after, x)),
        (below, to(lower, t, x)),
        (jnp.logical_and(below, has_before), to(lower, before, x)),
        (bridge_after, to(0, after, x)),
        (bridge_before, to(S - 1, before, x)),
    ):
        expected = expected + condition.astype(jnp.int32)

        @pl.when(condition)
        def _(device=device):
            pl.semaphore_signal(barrier, 1, device_id=device, device_id_type=pl.DeviceIdType.MESH)

    for device in [
        *(to(seg, t, lax.rem(x + step, 4)) for step in range(1, 4)),
        *(to(seg, time_of(z, lax.rem(y + step, 4), core), x) for step in range(1, 4)),
        *(to(seg, time_of(lax.rem(z + step, 4), y, core), x) for step in (1, 3)),
    ]:
        pl.semaphore_signal(barrier, 1, device_id=device, device_id_type=pl.DeviceIdType.MESH)

    def put_features(target):
        target[...] = jnp.concatenate([feat_ref[0].astype(F32), feat_ref[1].astype(F32)], axis=2).astype(BF)

    def put_seeds(target):
        eye = lax.broadcasted_iota(jnp.int32, (8, 8), 0) == lax.broadcasted_iota(jnp.int32, (8, 8), 1)
        head = head_ref[...]
        for f in range(frames):
            for i in range(3):
                halves = []
                for n in range(2):
                    line = score_ref[n, i, f : f + 1, :]
                    valid = jnp.where(t * frames + f < clip_ref[n], 1.0, 0.0)
                    stood = jnp.sum(jnp.where(eye, jnp.broadcast_to(line, (8, 8)), 0.0), axis=1, keepdims=True)
                    halves.append((stood * valid) * head)
                target[f, i] = jnp.concatenate(halves, axis=0).astype(BF)

    for load in loads:
        load.wait()

    @pl.when(seg == 0)
    def _():
        put_features(xin.at[pl.ds(frames, frames)])

    @pl.when(seg == S - 1)
    def _():
        put_features(own)
        put_seeds(din.at[pl.ds(0, frames)])

    pl.semaphore_wait(barrier, expected)
    pl.semaphore_signal(
        ready, 1, device_id=to(seg, time_of(lax.rem(z + 3, 4), y, core), x), device_id_type=pl.DeviceIdType.MESH
    )

    own_x = remote(xin.at[pl.ds(frames, frames)], xin.at[pl.ds(0, frames)], 0, 0, to(seg, after, x))
    own_d = remote(din.at[pl.ds(0, frames)], din.at[pl.ds(frames, frames)], 1, 1, to(seg, before, x))
    seam_x = remote(own, xin.at[pl.ds(0, frames)], 0, 0, to(0, after, x))
    seam_d = remote(own, din.at[pl.ds(frames, frames)], 1, 1, to(S - 1, before, x))
    x_up, d_down = [], []
    for h in range(2):
        here, later = pl.ds(2 * h, 2), pl.ds(frames + 2 * h, 2)
        x_up.append((
            remote(out_ref.at[here], xin.at[later], 2 + h, 2 + h, to(upper, t, x)),
            remote(out_ref.at[here], xin.at[here], 4 + h, 4 + h, to(upper, after, x)),
        ))
        d_down.append((
            remote(back_ref.at[here], din.at[here], 6 + h, 6 + h, to(lower, t, x)),
            remote(back_ref.at[here], din.at[later], 8 + h, 8 + h, to(lower, before, x)),
        ))
    slope_back = remote(slope.at[pl.ds(0, 2)], slope.at[pl.ds(4, 2)], 10, 10, to(seg, before, x))
    partner = to(seg, t + 1 - 2 * core, x)
    v_swap = remote(vsend, vbuf.at[pl.ds(6 * core, 4)], 11, 11, partner)
    u_to_one = remote(din.at[pl.ds(0, 4)], upad.at[pl.ds(2, 4), pl.ds(1, 3)], 12, 12, partner)
    u_to_zero = remote(pcot, upad.at[pl.ds(8, 2), pl.ds(1, 3)], 12, 12, partner)
    plain_x = jnp.logical_and(seg == 0, jnp.logical_and(has_after, jnp.logical_not(seam_after)))
    plain_d = jnp.logical_and(seg == S - 1, jnp.logical_and(has_before, jnp.logical_not(seam_before)))

    @pl.when(plain_x)
    def _():
        own_x.start()

    @pl.when(bridge_after)
    def _():
        seam_x.start()

    @pl.when(plain_d)
    def _():
        own_d.start()

    def flip_all():
        def one(i, carry):
            source = pl.multiple_of(i * 128, 128)
            target = pl.multiple_of((26 - i) * 128, 128)
            for which in range(2):
                tap = weight[which, pl.ds(source, 128), :].astype(F32)
                flipped[which, pl.ds(target, 128), :] = tap.T.astype(BF)
            return carry

        lax.fori_loop(0, 27, one, 0)

    @pl.when(below)
    def _():
        flip_all()

    @pl.when(below)
    def _():
        for straight, _ in x_up:
            straight.wait_recv()

    @pl.when(jnp.logical_and(below, has_before))
    def _():
        for _, across in x_up:
            across.wait_recv()

    @pl.when(jnp.logical_and(seg == 0, has_before))
    def _():
        own_x.wait_recv()

    gain = gain_ref[...]
    wide = xin[...].astype(F32)
    root = lax.rsqrt(jnp.mean(wide * wide, axis=-1, keepdims=True) + norm_eps)
    normed = (wide * root * gain).astype(BF).astype(F32)
    fill(patch8, normed)
    pre = convolve(patch8, weight, 0, 6)
    sig = 1.0 / (1.0 + jnp.exp(-pre))
    hidden = (pre * sig).astype(BF).astype(F32)
    slope[0:4] = (sig * (1.0 + pre * (1.0 - sig)))[2:6]

    @pl.when(has_before)
    def _():
        slope_back.start()

    fill(patch6, hidden)
    vsend[...] = jnp.where(core == 0, hidden[0:4], normed[4:8]).astype(BF)
    vbuf[pl.ds(4 * core, 6)] = jnp.where(core == 0, normed[2:8], hidden).astype(BF)
    v_swap.start()
    for h in range(2):
        rows = slice(2 * h, 2 * h + 2)
        second = convolve(patch6, weight, 1, 2, 2 * h)
        out_ref[rows] = (xin[4 + 2 * h : 6 + 2 * h].astype(F32) + second).astype(BF)

        @pl.when(jnp.logical_and(above, has_after))
        def _(h=h):
            x_up[h][1].start()

        @pl.when(above)
        def _(h=h):
            x_up[h][0].start()

    def stand_up():
        v_swap.wait_recv()
        flat = vbuf[...].astype(F32)
        for e, shifted in enumerate(column_shifts(flat)):
            rows = jnp.concatenate([shifted.reshape(480, 128), jnp.zeros((32, 128), F32)], axis=0)
            vt[e * 128 : (e + 1) * 128, :] = rows.T.astype(BF)

    @pl.when(bridge_before)
    def _():
        put_seeds(own)
        seam_d.start()

    @pl.when(seg == 0)
    def _():
        flip_all()

    @pl.when(above)
    def _():
        stand_up()

    @pl.when(above)
    def _():
        for straight, _ in d_down:
            straight.wait_recv()

    @pl.when(core == 0)
    def _():
        u_to_one.start()

    @pl.when(core == 1)
    def _():
        upad[6:10, 1:4] = din[0:4]

    @pl.when(jnp.logical_and(above, has_after))
    def _():
        for _, across in d_down:
            across.wait_recv()

    @pl.when(jnp.logical_and(seg == S - 1, has_after))
    def _():
        own_d.wait_recv()

    fill(patch8, din[...].astype(F32))
    hidden_cot = convolve(patch8, flipped, 1, 6)

    @pl.when(has_after)
    def _():
        slope_back.wait_recv()

    pre_cot = (hidden_cot * slope[...]).astype(BF)

    @pl.when(core == 0)
    def _():
        upad[2:8, 1:4] = pre_cot

    @pl.when(core == 1)
    def _():
        pcot[...] = pre_cot[2:4]
        u_to_zero.start()

    fill(patch6, pre_cot.astype(F32))
    for h in range(2):
        rows = slice(2 * h, 2 * h + 2)
        normed_cot = convolve(patch6, flipped, 0, 2, 2 * h)
        wide = xin[4 + 2 * h : 6 + 2 * h].astype(F32)
        root = lax.rsqrt(jnp.mean(wide * wide, axis=-1, keepdims=True) + norm_eps)
        weighted = normed_cot * gain
        inner = jnp.mean(weighted * wide, axis=-1, keepdims=True)
        back_ref[rows] = (din[rows].astype(F32) + (root * weighted - wide * root * root * root * inner)).astype(BF)

        @pl.when(jnp.logical_and(below, has_before))
        def _(h=h):
            d_down[h][1].start()

        @pl.when(below)
        def _(h=h):
            d_down[h][0].start()

    @pl.when(seg == S - 1)
    def _():
        stand_up()

    def on_x(step):
        return to(seg, t, lax.rem(x + step, 4))

    def on_y(step):
        return to(seg, time_of(z, lax.rem(y + step, 4), core), x)

    first, other = (x, y), (y, x)
    on_first, on_other = (on_x, on_y), (on_y, on_x)

    def group_at(h, step):
        return pl.ds(lax.rem(first[h] + step, 4) * GROUP, GROUP)

    def band_at(h, step):
        return pl.ds(pl.multiple_of(64 * h + lax.rem(other[h] + step, 4) * BAND, BAND), BAND)

    def piece(h, j, k):
        return grad_ref.at[core, group_at(h, j), band_at(h, k)]

    @pl.when(core == 0)
    def _():
        u_to_zero.wait_recv()

    @pl.when(core == 1)
    def _():
        u_to_one.wait_recv()

    for a in range(3):
        for b in range(3):
            rows = upad[2 - a : 12 - a, 2 - b : 5 - b].reshape(480, 128)
            rows = jnp.concatenate([rows, jnp.zeros((32, 128), BF)], axis=0)
            part = jnp.dot(vt[...], rows, preferred_element_type=F32)
            gsend[9 * a + 3 * b : 9 * a + 3 * b + 3] = part.astype(BF).reshape(3, 128, 128)

    started = []

    def send(source, target, device):
        index = len(started)
        copy = remote(source, target, 13 + index, 13 + index, device)
        copy.start()
        started.append(copy)
        return copy

    scattered = {}
    for k in (1, 2, 3, 0):
        for j in range(1, 4):
            for h in range(2):
                scattered[h, j, k] = send(gsend.at[group_at(h, j), band_at(h, k)], r1.at[h, j - 1, k], on_first[h](j))
    banded, total = {}, [None, None]
    for k in (1, 2, 3, 0):
        for h in range(2):
            total[h] = gsend[group_at(h, 0), band_at(h, k)].astype(F32)
            for j in range(1, 4):
                scattered[h, j, k].wait_recv()
                total[h] = total[h] + r1[h, j - 1, k].astype(F32)
            if k > 0:
                s1[h, k - 1] = total[h].astype(BF)
                banded[h, k] = send(s1.at[h, k - 1], r2.at[h, k - 1], on_other[h](k))
    for h in range(2):
        for k in range(1, 4):
            banded[h, k].wait_recv()
            total[h] = total[h] + r2[h, k - 1].astype(F32)
        zbuf[z, h] = total[h].astype(BF)
    pl.semaphore_wait(ready, 1)
    crossed = [
        send(zbuf.at[z], zbuf.at[z], to(seg, time_of(lax.rem(z + k, 4), y, core), x)) for k in (2, 1, 3)
    ]
    for copy in crossed:
        copy.wait_recv()
    for h in range(2):
        summed = zbuf[0, h].astype(F32)
        for k in range(1, 4):
            summed = summed + zbuf[k, h].astype(F32)
        grad_ref[core, group_at(h, 0), band_at(h, 0)] = summed.astype(BF)

    over_other, over_first, over_pair = {}, {}, []
    for k in range(1, 4):
        for h in range(2):
            over_other[h, k] = send(piece(h, 0, 0), piece(h, 0, 0), on_other[h](k))
    for k in range(4):
        for h in range(2):
            if k > 0:
                over_other[h, k].wait_recv()
            held = piece(h, 0, (4 - k) % 4)
            for j in range(1, 4):
                over_first[h, j, k] = send(held, held, on_first[h](j))
            over_pair.append(send(held, held, partner))
    for k in range(4):
        for j in range(1, 4):
            for h in range(2):
                over_first[h, j, k].wait_recv()
                held = piece(h, 4 - j, (4 - k) % 4)
                over_pair.append(send(held, held, partner))
    for copy in over_pair:
        copy.wait_recv()

    for copy in started:
        copy.wait_send()
    v_swap.wait_send()

    @pl.when(core == 0)
    def _():
        u_to_one.wait_send()

    @pl.when(core == 1)
    def _():
        u_to_zero.wait_send()

    @pl.when(has_before)
    def _():
        slope_back.wait_send()

    @pl.when(plain_x)
    def _():
        own_x.wait_send()

    @pl.when(plain_d)
    def _():
        own_d.wait_send()

    @pl.when(bridge_after)
    def _():
        seam_x.wait_send()

    @pl.when(bridge_before)
    def _():
        seam_d.wait_send()

    for condition, copies in (
        (above, [straight for straight, _ in x_up]),
        (jnp.logical_and(above, has_after), [across for _, across in x_up]),
        (below, [straight for straight, _ in d_down]),
        (jnp.logical_and(below, has_before), [across for _, across in d_down]),
    ):

        @pl.when(condition)
        def _(copies=copies):
            for copy in copies:
                copy.wait_send()


def solution(mesh):
    S, T = mesh.shape["segment"], mesh.shape["tm"]
    Y = 4
    Z = T // (2 * Y)
    vmem, hbm = pl.BlockSpec(memory_space=pltpu.VMEM), pl.BlockSpec(memory_space=pltpu.HBM)
    cells = (FRAMES_HERE, 3, 16, 128)

    def body(features, score_cot, clip_frames, conv_weights, norm_gains, score_head):
        out, grad, back = pl.pallas_call(
            functools.partial(kernel, S, T, Y, Z),
            out_shape=(
                jax.ShapeDtypeStruct(cells, BF),
                jax.ShapeDtypeStruct((2, 28, 128, 128), BF),
                jax.ShapeDtypeStruct(cells, BF),
            ),
            in_specs=[
                hbm, hbm, hbm, hbm, hbm, hbm,
            ],
            out_specs=(vmem, vmem, vmem),
            scratch_shapes=[
                pltpu.VMEM((2, FRAMES_HERE, 3, 8, 128), BF),
                pltpu.VMEM((2, 3, FRAMES_HERE, 8), F32),
                pltpu.SMEM((2,), jnp.int32),
                pltpu.VMEM((1, 128), F32),
                pltpu.VMEM((1, 128), F32),
                pltpu.VMEM(cells, BF),
                pltpu.VMEM((2, 3456, 128), BF),
                pltpu.VMEM((2, 3456, 128), BF),
                pltpu.VMEM((8, 3, 16, 128), BF),
                pltpu.VMEM((8, 3, 16, 128), BF),
                pltpu.VMEM((6, 3, 16, 128), F32),
                pltpu.VMEM((8, 5, 16, 384), BF),
                pltpu.VMEM((6, 5, 16, 384), BF),
                pltpu.VMEM((4, 3, 16, 128), BF),
                pltpu.VMEM((10, 3, 16, 128), BF),
                pltpu.VMEM((384, 512), BF),
                pltpu.VMEM((12, 5, 16, 128), BF),
                pltpu.VMEM((2, 3, 16, 128), BF),
                pltpu.VMEM((28, 128, 128), BF),
                pltpu.VMEM((2, 3, 4, GROUP, BAND, 128), BF),
                pltpu.VMEM((2, 3, GROUP, BAND, 128), BF),
                pltpu.VMEM((2, 3, GROUP, BAND, 128), BF),
                pltpu.VMEM((4, 2, GROUP, BAND, 128), BF),
                pltpu.SemaphoreType.DMA((6,)),
                pltpu.SemaphoreType.DMA((SENDS,)),
                pltpu.SemaphoreType.DMA((SENDS,)),
                pltpu.SemaphoreType.REGULAR,
            ],
            compiler_params=pltpu.CompilerParams(
                collective_id=0, has_side_effects=True, vmem_limit_bytes=56 * 1024 * 1024
            ),
            cost_estimate=pl.CostEstimate(flops=10**9, bytes_accessed=6 * 10**6, transcendentals=10**5),
        )(features, jnp.transpose(score_cot, (0, 2, 1, 3)), clip_frames, conv_weights, norm_gains, score_head.reshape(1, 128))

        def split_clips(cells):
            return jnp.transpose(cells.reshape(FRAMES_HERE, 3, 2, 8, 128), (2, 0, 1, 3, 4))[None]

        return split_clips(out), grad[:, :27].reshape(1, 2, 3456, 128), split_clips(back)

    return jax.shard_map(
        body,
        mesh=mesh,
        in_specs=(
            P("dp", "tm", None, None, None),
            P("dp", "tm", None, None),
            P("dp"),
            P("segment", None, None, None),
            P("segment", None),
            P(),
        ),
        out_specs=(
            P("segment", "dp", "tm", None, None, None),
            P("segment", None, None, None),
            P("segment", "dp", "tm", None, None, None),
        ),
        check_vma=False,
    )
```

time: 109 us -> 99.1 us (0.909)
  Pallas kernels: 101 us -> 93.9 us
  local copies, waits for them, and re-layouts: 7.02 us -> 4.36 us
    pallas_call x1, Pallas kernels: 101 us -> 93.9 us  [body(): pl.pallas_call(functools.partial(kernel, S, T, Y, Z), out_shape=(jax.Shap...]
    unnamed x11 -> x0, local copies, waits for them, and re-layouts: 4.95 us -> none
    slice x1, local copies, waits for them, and re-layouts: 1.41 us -> 2.88 us  [body(): grad[:, :27].reshape(1, 2, 3456, 128)]
where the time goes in v2:
time: 99.1 us; the launch traced here: 98.9 us
  Pallas kernels  93.9 us (95%)
  local copies, waits for them, and re-layouts  4.36 us (4%)
    pallas_call x1, Pallas kernels, body(): pl.pallas_call(functools.partial(kernel, S, T, Y, Z), out_shape=(jax.Shap...  93.9 us
    slice x1, local copies, waits for them, and re-layouts, body(): grad[:, :27].reshape(1, 2, 3456, 128)  2.88 us

profile of v2, /device:TPU:1, one launch (start us, length us, event | category | flops | bytes accessed | tf_op | source)
XLA Modules:
  0.0 98.9 jit_solution(10045354624758368635)
XLA Ops:
  0.6 93.9 %shard_map.85 = (bf16[4,3,16,128]{3,2,1,0:T(8,128)(2,1)}, bf16[2,28,128,128]{3,2,1,0:T(8,128)(2,1)}, bf16[4,3,16,128]{3,2,1,0:T(8,128)(2,1)}) custom-call(bf16[2,4,3,8,128]{4,3,2,1,0:T(8,128)(2,1)} %feat_hbm.1, f32[2,3,4,8]{3,2,1,0:T(4,128)} %bitcast.18, s32[2]{0:T(128)} %clip_hbm.1, bf16[1,2,3456,128]{3,2,1,0:T(8,128)(2,1)} %weight_hbm.1, ...), custom_call_target="tpu_custom_call" | custom-call | flops 1000000000 | bytes 6000000 | tf_op jit(solution)/shard_map/pallas_call | solution.py:486
  94.5 1.5 %copy_bitcast_fusion = (bf16[1,2,4,3,8,128]{5,4,3,2,1,0:T(8,128)(2,1)}, bf16[1,2,4,3,8,128]{5,4,3,2,1,0:T(8,128)(2,1)}) fusion(bf16[4,3,16,128]{3,2,1,0:T(8,128)(2,1)} %get-tuple-element.6, bf16[4,3,16,128]{3,2,1,0:T(8,128)(2,1)} %get-tuple-element.8), kind=kLoop, calls=%fused_computation | loop fusion | bytes 196608 | tf_op jit(solution)/shard_map/broadcast_in_dim | solution.py:533
  96.0 2.9 %slice.3 = bf16[2,27,128,128]{3,2,1,0:T(8,128)(2,1)} slice(bf16[2,28,128,128]{3,2,1,0:T(8,128)(2,1)} %get-tuple-element.7), slice={[0:2], [0:27], [0:128], [0:128]} | slice | bytes 3538944 | tf_op jit(solution)/shard_map/slice | solution.py:535

commit v3 on v2

--- a/solution.py
+++ b/solution.py
@@ -524,10 +524,16 @@
                 pltpu.SemaphoreType.REGULAR,
             ],
             compiler_params=pltpu.CompilerParams(
-                collective_id=0, has_side_effects=True, vmem_limit_bytes=56 * 1024 * 1024
+                collective_id=0, has_side_effects=True, vmem_limit_bytes=40 * 1024 * 1024
             ),
             cost_estimate=pl.CostEstimate(flops=10**9, bytes_accessed=6 * 10**6, transcendentals=10**5),
-        )(features, jnp.transpose(score_cot, (0, 2, 1, 3)), clip_frames, conv_weights, norm_gains, score_head.reshape(1, 128))
+        )(*(
+            pltpu.with_memory_space_constraint(array, pltpu.HBM)
+            for array in (
+                features, jnp.transpose(score_cot, (0, 2, 1, 3)), clip_frames, conv_weights, norm_gains,
+                score_head.reshape(1, 128),
+            )
+        ))
 
         def split_clips(cells):
             return jnp.transpose(cells.reshape(FRAMES_HERE, 3, 2, 8, 128), (2, 0, 1, 3, 4))[None]

time: 99.1 us -> 95.4 us (0.963)
  local copies, waits for them, and re-layouts: 4.36 us -> 1.98 us
  Pallas kernels: 93.9 us -> 92.7 us
    slice x1, local copies, waits for them, and re-layouts: 2.88 us -> 1.32 us  [body(): grad[:, :27].reshape(1, 2, 3456, 128)]
    pallas_call x1, Pallas kernels: 93.9 us -> 92.7 us  [body(): pl.pallas_call(functools.partial(kernel, S, T, Y, Z), out_shape=(jax.Shap...]
where the time goes in v3:
time: 95.4 us; the launch traced here: 95.3 us
  Pallas kernels  92.7 us (97%)
  local copies, waits for them, and re-layouts  1.98 us (2%)
    pallas_call x1, Pallas kernels, body(): pl.pallas_call(functools.partial(kernel, S, T, Y, Z), out_shape=(jax.Shap...  92.7 us

profile of v3, /device:TPU:1, one launch (start us, length us, event | category | flops | bytes accessed | tf_op | source)
XLA Modules:
  0.0 95.3 jit_solution(13309993089637742110)
XLA Ops:
  0.6 92.7 %shard_map.85 = (bf16[4,3,16,128]{3,2,1,0:T(8,128)(2,1)S(1)}, bf16[2,28,128,128]{3,2,1,0:T(8,128)(2,1)S(1)}, bf16[4,3,16,128]{3,2,1,0:T(8,128)(2,1)S(1)}) custom-call(bf16[2,4,3,8,128]{4,3,2,1,0:T(8,128)(2,1)} %feat_hbm.1, f32[2,3,4,8]{3,2,1,0:T(4,128)} %bitcast.18, s32[2]{0:T(128)} %clip_hbm.1, bf16[1,2,3456,128]{3,2,1,0:T(8,128)(2,1)} %weight_hbm.1, ...), custom_call_target="tpu_custom_call" | custom-call | flops 1000000000 | bytes 6000000 | tf_op jit(solution)/shard_map/pallas_call | solution.py:486
  93.3 0.7 copy_bitcast_fusion
  94.0 1.3 %slice.3 = bf16[2,27,128,128]{3,2,1,0:T(8,128)(2,1)} slice(bf16[2,28,128,128]{3,2,1,0:T(8,128)(2,1)S(1)} %get-tuple-element.7), slice={[0:2], [0:27], [0:128], [0:128]} | slice | bytes 3538944 | tf_op jit(solution)/shard_map/slice | solution.py:541

commit v4 on v3

--- a/solution.py
+++ b/solution.py
@@ -24,10 +24,10 @@
     return [before.reshape(shape), values, after.reshape(shape)]
 
 
-def fill(patch_ref, values):
+def fill(patch_ref, values, at=0):
     frames = values.shape[0]
     for e, shifted in enumerate(column_shifts(values)):
-        patch_ref[:frames, 1:4, :, e * 128 : (e + 1) * 128] = shifted.astype(BF)
+        patch_ref[at : at + frames, 1:4, :, e * 128 : (e + 1) * 128] = shifted.astype(BF)
 
 
 def convolve(patch_ref, weight_ref, which, frames, at=0):
@@ -45,7 +45,7 @@
     S, T, Y, Z,
     feat_hbm, score_hbm, clip_hbm, weight_hbm, gain_hbm, head_hbm,
     out_ref, grad_ref, back_ref,
-    feat_ref, score_ref, clip_ref, gain_ref, head_ref, own, weight, flipped, xin, din, slope, patch8, patch6, vsend, vbuf, vt, upad, pcot, gsend, r1, s1, r2, zbuf,
+    feat_ref, score_ref, clip_ref, gain_ref, head_ref, own, weight, flipped, xin, din, slope, patch8, patch6, patchb, hcot, vsend, vbuf, vt, upad, pcot, gsend, r1, s1, r2, zbuf,
     local_sem, send_sem, recv_sem, ready,
 ):
     seg, t, x = lax.axis_index("segment"), lax.axis_index("tm"), lax.axis_index("dp")
@@ -80,6 +80,8 @@
     patch8[:, 4] = jnp.zeros_like(patch8[:, 4])
     patch6[:, 0] = jnp.zeros_like(patch6[:, 0])
     patch6[:, 4] = jnp.zeros_like(patch6[:, 4])
+    patchb[:, 0] = jnp.zeros_like(patchb[:, 0])
+    patchb[:, 4] = jnp.zeros_like(patchb[:, 4])
     upad[...] = jnp.zeros_like(upad)
     gsend[27] = jnp.zeros_like(gsend[27])
     has_before, has_after = t > 0, t < T - 1
@@ -87,6 +89,8 @@
     seam_before = jnp.logical_and(has_before, lax.rem(t, 2 * Y) == 0)
     bridge_after = jnp.logical_and(seg == S - 1, seam_after)
     bridge_before = jnp.logical_and(seg == 0, seam_before)
+    ahead_to = jnp.logical_and(seg == S - 2, has_before)
+    ahead_from = jnp.logical_and(seg == S - 1, has_after)
     below, above = seg > 0, seg < S - 1
     before, after = jnp.maximum(t - 1, 0), jnp.minimum(t + 1, T - 1)
     lower, upper = jnp.maximum(seg - 1, 0), jnp.minimum(seg + 1, S - 1)
@@ -98,6 +102,7 @@
     @pl.when(jnp.logical_not(has_after))
     def _():
         din[frames:] = jnp.zeros_like(din[frames:])
+        xin[8:10] = jnp.zeros_like(xin[8:10])
         slope[frames:] = jnp.zeros_like(slope[frames:])
 
     barrier = pltpu.get_barrier_semaphore()
@@ -111,6 +116,8 @@
         (jnp.logical_and(below, has_before), to(lower, before, x)),
         (bridge_after, to(0, after, x)),
         (bridge_before, to(S - 1, before, x)),
+        (ahead_to, to(S - 1, before, x)),
+        (ahead_from, to(S - 2, after, x)),
     ):
         expected = expected + condition.astype(jnp.int32)
 
@@ -158,6 +165,7 @@
         ready, 1, device_id=to(seg, time_of(lax.rem(z + 3, 4), y, core), x), device_id_type=pl.DeviceIdType.MESH
     )
 
+    x_ahead = remote(out_ref.at[pl.ds(0, 2)], xin.at[pl.ds(8, 2)], 110, 110, to(S - 1, before, x))
     own_x = remote(xin.at[pl.ds(frames, frames)], xin.at[pl.ds(0, frames)], 0, 0, to(seg, after, x))
     own_d = remote(din.at[pl.ds(0, frames)], din.at[pl.ds(frames, frames)], 1, 1, to(seg, before, x))
     seam_x = remote(own, xin.at[pl.ds(0, frames)], 0, 0, to(0, after, x))
@@ -208,6 +216,18 @@
     def _():
         flip_all()
 
+    def hidden_back():
+        fill(patch8, din[...].astype(F32))
+        hcot[...] = convolve(patch8, flipped, 1, 6)
+
+    @pl.when(jnp.logical_and(seg == S - 1, has_after))
+    def _():
+        own_d.wait_recv()
+
+    @pl.when(seg == S - 1)
+    def _():
+        hidden_back()
+
     @pl.when(below)
     def _():
         for straight, _ in x_up:
@@ -223,16 +243,33 @@
         own_x.wait_recv()
 
     gain = gain_ref[...]
-    wide = xin[...].astype(F32)
-    root = lax.rsqrt(jnp.mean(wide * wide, axis=-1, keepdims=True) + norm_eps)
-    normed = (wide * root * gain).astype(BF).astype(F32)
+
+    def normalize(values):
+        wide = values.astype(F32)
+        root = lax.rsqrt(jnp.mean(wide * wide, axis=-1, keepdims=True) + norm_eps)
+        return (wide * root * gain).astype(BF).astype(F32)
+
+    normed = normalize(xin[0:8])
     fill(patch8, normed)
     pre = convolve(patch8, weight, 0, 6)
     sig = 1.0 / (1.0 + jnp.exp(-pre))
     hidden = (pre * sig).astype(BF).astype(F32)
     slope[0:4] = (sig * (1.0 + pre * (1.0 - sig)))[2:6]
 
-    @pl.when(has_before)
+    @pl.when(ahead_from)
+    def _():
+        x_ahead.wait_recv()
+
+    @pl.when(seg == S - 1)
+    def _():
+        fill(patch8, normalize(xin[8:10]), 8)
+        later = convolve(patch8, weight, 0, 2, 6)
+        share = 1.0 / (1.0 + jnp.exp(-later))
+        slope[4:6] = share * (1.0 + later * (1.0 - share))
+
+    slope_to, slope_from = jnp.logical_and(above, has_before), jnp.logical_and(above, has_after)
+
+    @pl.when(slope_to)
     def _():
         slope_back.start()
 
@@ -240,18 +277,29 @@
     vsend[...] = jnp.where(core == 0, hidden[0:4], normed[4:8]).astype(BF)
     vbuf[pl.ds(4 * core, 6)] = jnp.where(core == 0, normed[2:8], hidden).astype(BF)
     v_swap.start()
-    for h in range(2):
-        rows = slice(2 * h, 2 * h + 2)
-        second = convolve(patch6, weight, 1, 2, 2 * h)
-        out_ref[rows] = (xin[4 + 2 * h : 6 + 2 * h].astype(F32) + second).astype(BF)
-
-        @pl.when(jnp.logical_and(above, has_after))
-        def _(h=h):
-            x_up[h][1].start()
-
-        @pl.when(above)
-        def _(h=h):
-            x_up[h][0].start()
+    def second_half():
+        for h in range(2):
+            rows = slice(2 * h, 2 * h + 2)
+            second = convolve(patch6, weight, 1, 2, 2 * h)
+            out_ref[rows] = (xin[4 + 2 * h : 6 + 2 * h].astype(F32) + second).astype(BF)
+
+            @pl.when(jnp.logical_and(above, has_after))
+            def _(h=h):
+                x_up[h][1].start()
+
+            @pl.when(above)
+            def _(h=h):
+                x_up[h][0].start()
+
+            if h == 0:
+
+                @pl.when(ahead_to)
+                def _():
+                    x_ahead.start()
+
+    @pl.when(above)
+    def _():
+        second_half()
 
     def stand_up():
         v_swap.wait_recv()
@@ -291,18 +339,15 @@
         for _, across in d_down:
             across.wait_recv()
 
-    @pl.when(jnp.logical_and(seg == S - 1, has_after))
-    def _():
-        own_d.wait_recv()
-
-    fill(patch8, din[...].astype(F32))
-    hidden_cot = convolve(patch8, flipped, 1, 6)
-
-    @pl.when(has_after)
+    @pl.when(above)
+    def _():
+        hidden_back()
+
+    @pl.when(slope_from)
     def _():
         slope_back.wait_recv()
 
-    pre_cot = (hidden_cot * slope[...]).astype(BF)
+    pre_cot = (hcot[...] * slope[...]).astype(BF)
 
     @pl.when(core == 0)
     def _():
@@ -313,26 +358,35 @@
         pcot[...] = pre_cot[2:4]
         u_to_zero.start()
 
-    fill(patch6, pre_cot.astype(F32))
-    for h in range(2):
-        rows = slice(2 * h, 2 * h + 2)
-        normed_cot = convolve(patch6, flipped, 0, 2, 2 * h)
-        wide = xin[4 + 2 * h : 6 + 2 * h].astype(F32)
-        root = lax.rsqrt(jnp.mean(wide * wide, axis=-1, keepdims=True) + norm_eps)
-        weighted = normed_cot * gain
-        inner = jnp.mean(weighted * wide, axis=-1, keepdims=True)
-        back_ref[rows] = (din[rows].astype(F32) + (root * weighted - wide * root * root * root * inner)).astype(BF)
-
-        @pl.when(jnp.logical_and(below, has_before))
-        def _(h=h):
-            d_down[h][1].start()
-
-        @pl.when(below)
-        def _(h=h):
-            d_down[h][0].start()
+    fill(patchb, pre_cot.astype(F32))
+
+    def input_back():
+        for h in range(2):
+            rows = slice(2 * h, 2 * h + 2)
+            normed_cot = convolve(patchb, flipped, 0, 2, 2 * h)
+            wide = xin[4 + 2 * h : 6 + 2 * h].astype(F32)
+            root = lax.rsqrt(jnp.mean(wide * wide, axis=-1, keepdims=True) + norm_eps)
+            weighted = normed_cot * gain
+            inner = jnp.mean(weighted * wide, axis=-1, keepdims=True)
+            back_ref[rows] = (din[rows].astype(F32) + (root * weighted - wide * root * root * root * inner)).astype(BF)
+
+            @pl.when(jnp.logical_and(below, has_before))
+            def _(h=h):
+                d_down[h][1].start()
+
+            @pl.when(below)
+            def _(h=h):
+                d_down[h][0].start()
+
+    postponed = jnp.logical_and(seg == 0, core == 1)
+
+    @pl.when(jnp.logical_not(postponed))
+    def _():
+        input_back()
 
     @pl.when(seg == S - 1)
     def _():
+        second_half()
         stand_up()
 
     def on_x(step):
@@ -382,6 +436,11 @@
         for j in range(1, 4):
             for h in range(2):
                 scattered[h, j, k] = send(gsend.at[group_at(h, j), band_at(h, k)], r1.at[h, j - 1, k], on_first[h](j))
+
+    @pl.when(postponed)
+    def _():
+        input_back()
+
     banded, total = {}, [None, None]
     for k in (1, 2, 3, 0):
         for h in range(2):
@@ -442,9 +501,13 @@
     def _():
         u_to_zero.wait_send()
 
-    @pl.when(has_before)
+    @pl.when(slope_to)
     def _():
         slope_back.wait_send()
+
+    @pl.when(ahead_to)
+    def _():
+        x_ahead.wait_send()
 
     @pl.when(plain_x)
     def _():
@@ -503,11 +566,13 @@
                 pltpu.VMEM(cells, BF),
                 pltpu.VMEM((2, 3456, 128), BF),
                 pltpu.VMEM((2, 3456, 128), BF),
-                pltpu.VMEM((8, 3, 16, 128), BF),
+                pltpu.VMEM((10, 3, 16, 128), BF),
                 pltpu.VMEM((8, 3, 16, 128), BF),
                 pltpu.VMEM((6, 3, 16, 128), F32),
-                pltpu.VMEM((8, 5, 16, 384), BF),
+                pltpu.VMEM((10, 5, 16, 384), BF),
                 pltpu.VMEM((6, 5, 16, 384), BF),
+                pltpu.VMEM((6, 5, 16, 384), BF),
+                pltpu.VMEM((6, 3, 16, 128), F32),
                 pltpu.VMEM((4, 3, 16, 128), BF),
                 pltpu.VMEM((10, 3, 16, 128), BF),
                 pltpu.VMEM((384, 512), BF),

time: 95.4 us -> 92.3 us (0.968)
  Pallas kernels: 92.7 us -> 89.5 us
    pallas_call x1, Pallas kernels: 92.7 us -> 89.5 us  [body(): pl.pallas_call(functools.partial(kernel, S, T, Y, Z), out_shape=(jax.Shap...]
where the time goes in v4:
time: 92.3 us; the launch traced here: 92.1 us
  Pallas kernels  89.5 us (97%)
  local copies, waits for them, and re-layouts  1.98 us (2%)
    pallas_call x1, Pallas kernels, body(): pl.pallas_call(functools.partial(kernel, S, T, Y, Z), out_shape=(jax.Shap...  89.5 us

profile of v4, /device:TPU:1, one launch (start us, length us, event | category | flops | bytes accessed | tf_op | source)
XLA Modules:
  0.0 92.1 jit_solution(14231074744788352868)
XLA Ops:
  0.6 89.5 %shard_map.85 = (bf16[4,3,16,128]{3,2,1,0:T(8,128)(2,1)S(1)}, bf16[2,28,128,128]{3,2,1,0:T(8,128)(2,1)S(1)}, bf16[4,3,16,128]{3,2,1,0:T(8,128)(2,1)S(1)}) custom-call(bf16[2,4,3,8,128]{4,3,2,1,0:T(8,128)(2,1)} %feat_hbm.1, f32[2,3,4,8]{3,2,1,0:T(4,128)} %bitcast.18, s32[2]{0:T(128)} %clip_hbm.1, bf16[1,2,3456,128]{3,2,1,0:T(8,128)(2,1)} %weight_hbm.1, ...), custom_call_target="tpu_custom_call" | custom-call | flops 1000000000 | bytes 6000000 | tf_op jit(solution)/shard_map/pallas_call | solution.py:549
  90.2 0.7 copy_bitcast_fusion
  90.8 1.3 %slice.3 = bf16[2,27,128,128]{3,2,1,0:T(8,128)(2,1)} slice(bf16[2,28,128,128]{3,2,1,0:T(8,128)(2,1)S(1)} %get-tuple-element.7), slice={[0:2], [0:27], [0:128], [0:128]} | slice | bytes 3538944 | tf_op jit(solution)/shard_map/slice | solution.py:606

commit v5 on v4

--- a/solution.py
+++ b/solution.py
@@ -30,22 +30,24 @@
         patch_ref[at : at + frames, 1:4, :, e * 128 : (e + 1) * 128] = shifted.astype(BF)
 
 
-def convolve(patch_ref, weight_ref, which, frames, at=0):
-    total = None
-    for a in range(3):
-        for b in range(3):
-            rows = patch_ref[at + a : at + a + frames, b : b + 3].reshape(frames * 48, 384)
-            taps = weight_ref[which, (9 * a + 3 * b) * 128 : (9 * a + 3 * b + 3) * 128, :]
-            part = jnp.dot(rows, taps, preferred_element_type=F32)
-            total = part if total is None else total + part
-    return total.reshape(frames, 3, 16, 128)
+def convolve(patch_ref, weights, which, frames, at=0):
+    early_ref, late_ref = weights
+
+    def rows(start, count):
+        bands = [patch_ref[start : start + count, b : b + 3].reshape(count * 48, 384) for b in range(3)]
+        return jnp.concatenate(bands, axis=1)
+
+    early = jnp.dot(rows(at, frames + 1), early_ref[which], preferred_element_type=F32)
+    early = early.reshape(frames + 1, 3, 16, 256)
+    late = jnp.dot(rows(at + 2, frames), late_ref[which], preferred_element_type=F32)
+    return early[:frames, ..., :128] + early[1:, ..., 128:] + late.reshape(frames, 3, 16, 128)
 
 
 def kernel(
     S, T, Y, Z,
     feat_hbm, score_hbm, clip_hbm, weight_hbm, gain_hbm, head_hbm,
     out_ref, grad_ref, back_ref,
-    feat_ref, score_ref, clip_ref, gain_ref, head_ref, own, weight, flipped, xin, din, slope, patch8, patch6, patchb, hcot, vsend, vbuf, vt, upad, pcot, gsend, r1, s1, r2, zbuf,
+    feat_ref, score_ref, clip_ref, gain_ref, head_ref, own, early, late, early_flip, late_flip, xin, din, slope, patch8, patch6, patchb, hcot, vsend, vbuf, vt, upad, pcot, gsend, r1, s1, r2, zbuf,
     local_sem, send_sem, recv_sem, ready,
 ):
     seg, t, x = lax.axis_index("segment"), lax.axis_index("tm"), lax.axis_index("dp")
@@ -69,12 +71,17 @@
     loads = [
         pltpu.make_async_copy(source, target, local_sem.at[i])
         for i, (source, target) in enumerate((
-            (feat_hbm, feat_ref), (gain_hbm, gain_ref), (weight_hbm.at[0], weight),
+            (feat_hbm, feat_ref), (gain_hbm, gain_ref),
+            (weight_hbm.at[0, :, pl.ds(0, 1152)], early.at[:, :, pl.ds(0, 128)]),
+            (weight_hbm.at[0, :, pl.ds(1152, 1152)], early.at[:, :, pl.ds(128, 128)]),
+            (weight_hbm.at[0, :, pl.ds(2304, 1152)], late),
             (score_hbm, score_ref), (clip_hbm, clip_ref), (head_hbm, head_ref),
         ))
     ]
     for load in loads:
         load.start()
+
+    weight, flipped = (early, late), (early_flip, late_flip)
 
     patch8[:, 0] = jnp.zeros_like(patch8[:, 0])
     patch8[:, 4] = jnp.zeros_like(patch8[:, 4])
@@ -202,15 +209,21 @@
         own_d.start()
 
     def flip_all():
+        first, middle = pl.ds(0, 128), pl.ds(128, 128)
+        pairs = (
+            (early, first, late_flip, first), (early, middle, early_flip, middle), (late, first, early_flip, first),
+        )
+
         def one(i, carry):
-            source = pl.multiple_of(i * 128, 128)
-            target = pl.multiple_of((26 - i) * 128, 128)
-            for which in range(2):
-                tap = weight[which, pl.ds(source, 128), :].astype(F32)
-                flipped[which, pl.ds(target, 128), :] = tap.T.astype(BF)
+            source = pl.ds(pl.multiple_of(i * 128, 128), 128)
+            target = pl.ds(pl.multiple_of((8 - i) * 128, 128), 128)
+            for from_ref, from_columns, to_ref, to_columns in pairs:
+                for which in range(2):
+                    tap = from_ref[which, source, from_columns].astype(F32)
+                    to_ref[which, target, to_columns] = tap.T.astype(BF)
             return carry
 
-        lax.fori_loop(0, 27, one, 0)
+        lax.fori_loop(0, 9, one, 0)
 
     @pl.when(below)
     def _():
@@ -415,12 +428,15 @@
     def _():
         u_to_one.wait_recv()
 
-    for a in range(3):
-        for b in range(3):
+    taps = [(a, b) for a in range(3) for b in range(3)]
+    for start in range(0, 9, 2):
+        columns = []
+        for a, b in taps[start : start + 2]:
             rows = upad[2 - a : 12 - a, 2 - b : 5 - b].reshape(480, 128)
-            rows = jnp.concatenate([rows, jnp.zeros((32, 128), BF)], axis=0)
-            part = jnp.dot(vt[...], rows, preferred_element_type=F32)
-            gsend[9 * a + 3 * b : 9 * a + 3 * b + 3] = part.astype(BF).reshape(3, 128, 128)
+            columns.append(jnp.concatenate([rows, jnp.zeros((32, 128), BF)], axis=0))
+        part = jnp.dot(vt[...], jnp.concatenate(columns, axis=1), preferred_element_type=F32).astype(BF)
+        for n, (a, b) in enumerate(taps[start : start + 2]):
+            gsend[9 * a + 3 * b : 9 * a + 3 * b + 3] = part[:, n * 128 : (n + 1) * 128].reshape(3, 128, 128)
 
     started = []
 
@@ -564,8 +580,10 @@
                 pltpu.VMEM((1, 128), F32),
                 pltpu.VMEM((1, 128), F32),
                 pltpu.VMEM(cells, BF),
-                pltpu.VMEM((2, 3456, 128), BF),
-                pltpu.VMEM((2, 3456, 128), BF),
+                pltpu.VMEM((2, 1152, 256), BF),
+                pltpu.VMEM((2, 1152, 128), BF),
+                pltpu.VMEM((2, 1152, 256), BF),
+                pltpu.VMEM((2, 1152, 128), BF),
                 pltpu.VMEM((10, 3, 16, 128), BF),
                 pltpu.VMEM((8, 3, 16, 128), BF),
                 pltpu.VMEM((6, 3, 16, 128), F32),
@@ -583,7 +601,7 @@
                 pltpu.VMEM((2, 3, GROUP, BAND, 128), BF),
                 pltpu.VMEM((2, 3, GROUP, BAND, 128), BF),
                 pltpu.VMEM((4, 2, GROUP, BAND, 128), BF),
-                pltpu.SemaphoreType.DMA((6,)),
+                pltpu.SemaphoreType.DMA((8,)),
                 pltpu.SemaphoreType.DMA((SENDS,)),
                 pltpu.SemaphoreType.DMA((SENDS,)),
                 pltpu.SemaphoreType.REGULAR,

time: 92.3 us -> 91.1 us (0.987)
  Pallas kernels: 89.5 us -> 88.3 us
    pallas_call x1, Pallas kernels: 89.5 us -> 88.3 us  [body(): pl.pallas_call(functools.partial(kernel, S, T, Y, Z), out_shape=(jax.Shap...]
where the time goes in v5:
time: 91.1 us; the launch traced here: 90.9 us
  Pallas kernels  88.3 us (97%)
  local copies, waits for them, and re-layouts  1.98 us (2%)
    pallas_call x1, Pallas kernels, body(): pl.pallas_call(functools.partial(kernel, S, T, Y, Z), out_shape=(jax.Shap...  88.3 us

profile of v5, /device:TPU:1, one launch (start us, length us, event | category | flops | bytes accessed | tf_op | source)
XLA Modules:
  0.0 90.9 jit_solution(14553438218765833691)
XLA Ops:
  0.6 88.3 %shard_map.85 = (bf16[4,3,16,128]{3,2,1,0:T(8,128)(2,1)S(1)}, bf16[2,28,128,128]{3,2,1,0:T(8,128)(2,1)S(1)}, bf16[4,3,16,128]{3,2,1,0:T(8,128)(2,1)S(1)}) custom-call(bf16[2,4,3,8,128]{4,3,2,1,0:T(8,128)(2,1)} %feat_hbm.1, f32[2,3,4,8]{3,2,1,0:T(4,128)} %bitcast.18, s32[2]{0:T(128)} %clip_hbm.1, bf16[1,2,3456,128]{3,2,1,0:T(8,128)(2,1)} %weight_hbm.1, ...), custom_call_target="tpu_custom_call" | custom-call | flops 1000000000 | bytes 6000000 | tf_op jit(solution)/shard_map/pallas_call | solution.py:565
  89.0 0.7 copy_bitcast_fusion
  89.6 1.3 %slice.3 = bf16[2,27,128,128]{3,2,1,0:T(8,128)(2,1)} slice(bf16[2,28,128,128]{3,2,1,0:T(8,128)(2,1)S(1)} %get-tuple-element.7), slice={[0:2], [0:27], [0:128], [0:128]} | slice | bytes 3538944 | tf_op jit(solution)/shard_map/slice | solution.py:624

commit v6 on v5

--- a/solution.py
+++ b/solution.py
@@ -11,7 +11,7 @@
 FRAMES_HERE = 4
 GROUP = 7
 BAND = 16
-SENDS = 112
+SENDS = 116
 BF, F32 = jnp.bfloat16, jnp.float32
 
 
@@ -47,7 +47,7 @@
     S, T, Y, Z,
     feat_hbm, score_hbm, clip_hbm, weight_hbm, gain_hbm, head_hbm,
     out_ref, grad_ref, back_ref,
-    feat_ref, score_ref, clip_ref, gain_ref, head_ref, own, early, late, early_flip, late_flip, xin, din, slope, patch8, patch6, patchb, hcot, vsend, vbuf, vt, upad, pcot, gsend, r1, s1, r2, zbuf,
+    feat_ref, score_ref, clip_ref, gain_ref, head_ref, own, early, late, early_flip, late_flip, xin, din, slope, patch8, patch6, patchb, hcot, roots, vsend, vbuf, vt, upad, pcot, gsend, r1, s1, r2, zbuf,
     local_sem, send_sem, recv_sem, ready,
 ):
     seg, t, x = lax.axis_index("segment"), lax.axis_index("tm"), lax.axis_index("dp")
@@ -71,11 +71,11 @@
     loads = [
         pltpu.make_async_copy(source, target, local_sem.at[i])
         for i, (source, target) in enumerate((
-            (feat_hbm, feat_ref), (gain_hbm, gain_ref),
+            (feat_hbm, feat_ref), (score_hbm, score_ref), (clip_hbm, clip_ref), (head_hbm, head_ref),
+            (gain_hbm, gain_ref),
             (weight_hbm.at[0, :, pl.ds(0, 1152)], early.at[:, :, pl.ds(0, 128)]),
             (weight_hbm.at[0, :, pl.ds(1152, 1152)], early.at[:, :, pl.ds(128, 128)]),
             (weight_hbm.at[0, :, pl.ds(2304, 1152)], late),
-            (score_hbm, score_ref), (clip_hbm, clip_ref), (head_hbm, head_ref),
         ))
     ]
     for load in loads:
@@ -83,14 +83,6 @@
 
     weight, flipped = (early, late), (early_flip, late_flip)
 
-    patch8[:, 0] = jnp.zeros_like(patch8[:, 0])
-    patch8[:, 4] = jnp.zeros_like(patch8[:, 4])
-    patch6[:, 0] = jnp.zeros_like(patch6[:, 0])
-    patch6[:, 4] = jnp.zeros_like(patch6[:, 4])
-    patchb[:, 0] = jnp.zeros_like(patchb[:, 0])
-    patchb[:, 4] = jnp.zeros_like(patchb[:, 4])
-    upad[...] = jnp.zeros_like(upad)
-    gsend[27] = jnp.zeros_like(gsend[27])
     has_before, has_after = t > 0, t < T - 1
     seam_after = jnp.logical_and(has_after, lax.rem(t, 2 * Y) == 2 * Y - 1)
     seam_before = jnp.logical_and(has_before, lax.rem(t, 2 * Y) == 0)
@@ -101,16 +93,6 @@
     below, above = seg > 0, seg < S - 1
     before, after = jnp.maximum(t - 1, 0), jnp.minimum(t + 1, T - 1)
     lower, upper = jnp.maximum(seg - 1, 0), jnp.minimum(seg + 1, S - 1)
-
-    @pl.when(jnp.logical_not(has_before))
-    def _():
-        xin[0:frames] = jnp.zeros_like(xin[0:frames])
-
-    @pl.when(jnp.logical_not(has_after))
-    def _():
-        din[frames:] = jnp.zeros_like(din[frames:])
-        xin[8:10] = jnp.zeros_like(xin[8:10])
-        slope[frames:] = jnp.zeros_like(slope[frames:])
 
     barrier = pltpu.get_barrier_semaphore()
     expected = 8
@@ -139,6 +121,27 @@
     ]:
         pl.semaphore_signal(barrier, 1, device_id=device, device_id_type=pl.DeviceIdType.MESH)
 
+    patch8[:, 0] = jnp.zeros_like(patch8[:, 0])
+    patch8[:, 4] = jnp.zeros_like(patch8[:, 4])
+    patch6[:, 0] = jnp.zeros_like(patch6[:, 0])
+    patch6[:, 4] = jnp.zeros_like(patch6[:, 4])
+    patchb[:, 0] = jnp.zeros_like(patchb[:, 0])
+    patchb[:, 4] = jnp.zeros_like(patchb[:, 4])
+    upad[:, 0] = jnp.zeros_like(upad[:, 0])
+    upad[:, 4] = jnp.zeros_like(upad[:, 4])
+    upad[0:2, 1:4] = jnp.zeros_like(upad[0:2, 1:4])
+    upad[10:12, 1:4] = jnp.zeros_like(upad[10:12, 1:4])
+    gsend[27] = jnp.zeros_like(gsend[27])
+    @pl.when(jnp.logical_not(has_before))
+    def _():
+        xin[0:frames] = jnp.zeros_like(xin[0:frames])
+
+    @pl.when(jnp.logical_not(has_after))
+    def _():
+        din[frames:] = jnp.zeros_like(din[frames:])
+        xin[8:10] = jnp.zeros_like(xin[8:10])
+        slope[frames:] = jnp.zeros_like(slope[frames:])
+
     def put_features(target):
         target[...] = jnp.concatenate([feat_ref[0].astype(F32), feat_ref[1].astype(F32)], axis=2).astype(BF)
 
@@ -155,7 +158,7 @@
                     halves.append((stood * valid) * head)
                 target[f, i] = jnp.concatenate(halves, axis=0).astype(BF)
 
-    for load in loads:
+    for load in loads[:5]:
         load.wait()
 
     @pl.when(seg == 0)
@@ -172,7 +175,7 @@
         ready, 1, device_id=to(seg, time_of(lax.rem(z + 3, 4), y, core), x), device_id_type=pl.DeviceIdType.MESH
     )
 
-    x_ahead = remote(out_ref.at[pl.ds(0, 2)], xin.at[pl.ds(8, 2)], 110, 110, to(S - 1, before, x))
+    x_ahead = remote(out_ref.at[pl.ds(0, 2)], xin.at[pl.ds(8, 2)], 115, 115, to(S - 1, before, x))
     own_x = remote(xin.at[pl.ds(frames, frames)], xin.at[pl.ds(0, frames)], 0, 0, to(seg, after, x))
     own_d = remote(din.at[pl.ds(0, frames)], din.at[pl.ds(frames, frames)], 1, 1, to(seg, before, x))
     seam_x = remote(own, xin.at[pl.ds(0, frames)], 0, 0, to(0, after, x))
@@ -208,6 +211,9 @@
     def _():
         own_d.start()
 
+    for load in loads[5:]:
+        load.wait()
+
     def flip_all():
         first, middle = pl.ds(0, 128), pl.ds(128, 128)
         pairs = (
@@ -260,9 +266,10 @@
     def normalize(values):
         wide = values.astype(F32)
         root = lax.rsqrt(jnp.mean(wide * wide, axis=-1, keepdims=True) + norm_eps)
-        return (wide * root * gain).astype(BF).astype(F32)
-
-    normed = normalize(xin[0:8])
+        return (wide * root * gain).astype(BF).astype(F32), root
+
+    normed, root = normalize(xin[0:8])
+    roots[...] = jnp.broadcast_to(root[4:8], roots.shape)
     fill(patch8, normed)
     pre = convolve(patch8, weight, 0, 6)
     sig = 1.0 / (1.0 + jnp.exp(-pre))
@@ -275,7 +282,7 @@
 
     @pl.when(seg == S - 1)
     def _():
-        fill(patch8, normalize(xin[8:10]), 8)
+        fill(patch8, normalize(xin[8:10])[0], 8)
         later = convolve(patch8, weight, 0, 2, 6)
         share = 1.0 / (1.0 + jnp.exp(-later))
         slope[4:6] = share * (1.0 + later * (1.0 - share))
@@ -378,7 +385,7 @@
             rows = slice(2 * h, 2 * h + 2)
             normed_cot = convolve(patchb, flipped, 0, 2, 2 * h)
             wide = xin[4 + 2 * h : 6 + 2 * h].astype(F32)
-            root = lax.rsqrt(jnp.mean(wide * wide, axis=-1, keepdims=True) + norm_eps)
+            root = roots[rows]
             weighted = normed_cot * gain
             inner = jnp.mean(weighted * wide, axis=-1, keepdims=True)
             back_ref[rows] = (din[rows].astype(F32) + (root * weighted - wide * root * root * root * inner)).astype(BF)
@@ -467,15 +474,63 @@
             if k > 0:
                 s1[h, k - 1] = total[h].astype(BF)
                 banded[h, k] = send(s1.at[h, k - 1], r2.at[h, k - 1], on_other[h](k))
+    crossed = []
     for h in range(2):
         for k in range(1, 4):
             banded[h, k].wait_recv()
             total[h] = total[h] + r2[h, k - 1].astype(F32)
         zbuf[z, h] = total[h].astype(BF)
-    pl.semaphore_wait(ready, 1)
-    crossed = [
-        send(zbuf.at[z], zbuf.at[z], to(seg, time_of(lax.rem(z + k, 4), y, core), x)) for k in (2, 1, 3)
-    ]
+        for k in (2, 1, 3):
+            if h == 0 and k == 2:
+                pl.semaphore_wait(ready, 1)
+            crossed.append(send(zbuf.at[z, h], zbuf.at[z, h], to(seg, time_of(lax.rem(z + k, 4), y, core), x)))
+    v_swap.wait_send()
+
+    @pl.when(core == 0)
+    def _():
+        u_to_one.wait_send()
+
+    @pl.when(core == 1)
+    def _():
+        u_to_zero.wait_send()
+
+    @pl.when(slope_to)
+    def _():
+        slope_back.wait_send()
+
+    @pl.when(ahead_to)
+    def _():
+        x_ahead.wait_send()
+
+    @pl.when(plain_x)
+    def _():
+        own_x.wait_send()
+
+    @pl.when(plain_d)
+    def _():
+        own_d.wait_send()
+
+    @pl.when(bridge_after)
+    def _():
+        seam_x.wait_send()
+
+    @pl.when(bridge_before)
+    def _():
+        seam_d.wait_send()
+
+    for condition, copies in (
+        (above, [straight for straight, _ in x_up]),
+        (jnp.logical_and(above, has_after), [across for _, across in x_up]),
+        (below, [straight for straight, _ in d_down]),
+        (jnp.logical_and(below, has_before), [across for _, across in d_down]),
+    ):
+
+        @pl.when(condition)
+        def _(copies=copies):
+            for copy in copies:
+                copy.wait_send()
+    for copy in started:
+        copy.wait_send()
     for copy in crossed:
         copy.wait_recv()
     for h in range(2):
@@ -502,56 +557,13 @@
                 over_first[h, j, k].wait_recv()
                 held = piece(h, 4 - j, (4 - k) % 4)
                 over_pair.append(send(held, held, partner))
+    for copy in [*over_other.values(), *over_first.values()]:
+        copy.wait_send()
     for copy in over_pair:
         copy.wait_recv()
 
-    for copy in started:
+    for copy in over_pair:
         copy.wait_send()
-    v_swap.wait_send()
-
-    @pl.when(core == 0)
-    def _():
-        u_to_one.wait_send()
-
-    @pl.when(core == 1)
-    def _():
-        u_to_zero.wait_send()
-
-    @pl.when(slope_to)
-    def _():
-        slope_back.wait_send()
-
-    @pl.when(ahead_to)
-    def _():
-        x_ahead.wait_send()
-
-    @pl.when(plain_x)
-    def _():
-        own_x.wait_send()
-
-    @pl.when(plain_d)
-    def _():
-        own_d.wait_send()
-
-    @pl.when(bridge_after)
-    def _():
-        seam_x.wait_send()
-
-    @pl.when(bridge_before)
-    def _():
-        seam_d.wait_send()
-
-    for condition, copies in (
-        (above, [straight for straight, _ in x_up]),
-        (jnp.logical_and(above, has_after), [across for _, across in x_up]),
-        (below, [straight for straight, _ in d_down]),
-        (jnp.logical_and(below, has_before), [across for _, across in d_down]),
-    ):
-
-        @pl.when(condition)
-        def _(copies=copies):
-            for copy in copies:
-                copy.wait_send()
 
 
 def solution(mesh):
@@ -591,6 +603,7 @@
                 pltpu.VMEM((6, 5, 16, 384), BF),
                 pltpu.VMEM((6, 5, 16, 384), BF),
                 pltpu.VMEM((6, 3, 16, 128), F32),
+                pltpu.VMEM(cells, F32),
                 pltpu.VMEM((4, 3, 16, 128), BF),
                 pltpu.VMEM((10, 3, 16, 128), BF),
                 pltpu.VMEM((384, 512), BF),

time: 91.1 us -> 90.6 us (level)
  no operation moved by 1% of the time
where the time goes in v6:
time: 90.6 us; the launch traced here: 90.5 us
  Pallas kernels  87.9 us (97%)
  local copies, waits for them, and re-layouts  1.98 us (2%)
    pallas_call x1, Pallas kernels, body(): pl.pallas_call(functools.partial(kernel, S, T, Y, Z), out_shape=(jax.Shap...  87.9 us

profile of v6, /device:TPU:1, one launch (start us, length us, event | category | flops | bytes accessed | tf_op | source)
XLA Modules:
  0.0 90.5 jit_solution(5957044040282506787)
XLA Ops:
  0.6 87.9 %shard_map.85 = (bf16[4,3,16,128]{3,2,1,0:T(8,128)(2,1)S(1)}, bf16[2,28,128,128]{3,2,1,0:T(8,128)(2,1)S(1)}, bf16[4,3,16,128]{3,2,1,0:T(8,128)(2,1)S(1)}) custom-call(bf16[2,4,3,8,128]{4,3,2,1,0:T(8,128)(2,1)} %feat_hbm.1, f32[2,3,4,8]{3,2,1,0:T(4,128)} %bitcast.18, s32[2]{0:T(128)} %clip_hbm.1, bf16[1,2,3456,128]{3,2,1,0:T(8,128)(2,1)} %weight_hbm.1, ...), custom_call_target="tpu_custom_call" | custom-call | flops 1000000000 | bytes 6000000 | tf_op jit(solution)/shard_map/pallas_call | solution.py:577
  88.5 0.7 copy_bitcast_fusion
  89.2 1.3 %slice.3 = bf16[2,27,128,128]{3,2,1,0:T(8,128)(2,1)} slice(bf16[2,28,128,128]{3,2,1,0:T(8,128)(2,1)S(1)} %get-tuple-element.7), slice={[0:2], [0:27], [0:128], [0:128]} | slice | bytes 3538944 | tf_op jit(solution)/shard_map/slice | solution.py:637

commit v7 on v6

--- a/solution.py
+++ b/solution.py
@@ -456,7 +456,7 @@
 
     scattered = {}
     for k in (1, 2, 3, 0):
-        for j in range(1, 4):
+        for j in (2, 1, 3):
             for h in range(2):
                 scattered[h, j, k] = send(gsend.at[group_at(h, j), band_at(h, k)], r1.at[h, j - 1, k], on_first[h](j))
 
@@ -540,7 +540,7 @@
         grad_ref[core, group_at(h, 0), band_at(h, 0)] = summed.astype(BF)
 
     over_other, over_first, over_pair = {}, {}, []
-    for k in range(1, 4):
+    for k in (2, 1, 3):
         for h in range(2):
             over_other[h, k] = send(piece(h, 0, 0), piece(h, 0, 0), on_other[h](k))
     for k in range(4):
@@ -548,7 +548,7 @@
             if k > 0:
                 over_other[h, k].wait_recv()
             held = piece(h, 0, (4 - k) % 4)
-            for j in range(1, 4):
+            for j in (2, 1, 3):
                 over_first[h, j, k] = send(held, held, on_first[h](j))
             over_pair.append(send(held, held, partner))
     for k in range(4):

time: 90.6 us -> 90.2 us (level)
  no operation moved by 1% of the time
where the time goes in v7:
time: 90.2 us; the launch traced here: 90 us
  Pallas kernels  87.4 us (97%)
  local copies, waits for them, and re-layouts  1.98 us (2%)
    pallas_call x1, Pallas kernels, body(): pl.pallas_call(functools.partial(kernel, S, T, Y, Z), out_shape=(jax.Shap...  87.4 us

profile of v7, /device:TPU:1, one launch (start us, length us, event | category | flops | bytes accessed | tf_op | source)
XLA Modules:
  0.0 90.0 jit_solution(11502136754626821104)
XLA Ops:
  0.6 87.4 %shard_map.85 = (bf16[4,3,16,128]{3,2,1,0:T(8,128)(2,1)S(1)}, bf16[2,28,128,128]{3,2,1,0:T(8,128)(2,1)S(1)}, bf16[4,3,16,128]{3,2,1,0:T(8,128)(2,1)S(1)}) custom-call(bf16[2,4,3,8,128]{4,3,2,1,0:T(8,128)(2,1)} %feat_hbm.1, f32[2,3,4,8]{3,2,1,0:T(4,128)} %bitcast.18, s32[2]{0:T(128)} %clip_hbm.1, bf16[1,2,3456,128]{3,2,1,0:T(8,128)(2,1)} %weight_hbm.1, ...), custom_call_target="tpu_custom_call" | custom-call | flops 1000000000 | bytes 6000000 | tf_op jit(solution)/shard_map/pallas_call | solution.py:577
  88.1 0.7 copy_bitcast_fusion
  88.7 1.3 %slice.3 = bf16[2,27,128,128]{3,2,1,0:T(8,128)(2,1)} slice(bf16[2,28,128,128]{3,2,1,0:T(8,128)(2,1)S(1)} %get-tuple-element.7), slice={[0:2], [0:27], [0:128], [0:128]} | slice | bytes 3538944 | tf_op jit(solution)/shard_map/slice | solution.py:637
